TPU v7x, 32 devices: a whole 2x2x4 slice. The times are simulated.
32 devices in a mesh: row: 8 (over z, core), col: 4 (over y, x).
Axes of the slice: x: 2, y: 2, z: 4, core: 2. Of those that a mesh axis runs over, the one named last changes fastest.
Arguments:
- centroids: float32 [3, 1024], P(None, ('row', 'col')), may hold values from -4 to 4
- strengths: float32 [32, 1024], P(None, ('row', 'col')), may hold values from -6 to 6
- self_inv: float32 [32, 1024], P(None, ('row', 'col')), may hold values from -6 to 6
- wavenumbers: float32 [16], replicated, may hold values from 0.3 to 2
- field_pos: float32 [3, 2048], P(None, 'row'), may hold values from -4 to 4
- targets: float32 [32, 2048], P(None, 'row'), may hold values from -6 to 6
- lists: int32 [2048, 64], P('row'), may hold values from 0 to 1023
- connect: int32 [4, 1024], P(None, 'row'), may hold values from 0 to 1023, as said below
Outputs:
- adjoint: float32 [32, 1024], P(None, ('row', 'col'))
- vertex_sens: float32 [3, 1024], P(None, ('row', 'col'))
- objective: float32 [], replicated
Inputs may be any that keep to these rules, and one draw needn't show every extreme that they name: `connect`: the four vertices of panel i lie in the block of 128 vertices that starts at i - i % 128; the first of them is i itself.
All inputs are finite; a program needn't handle non-finite values.
Results may differ from a plain program's by a relative error of at most 0.0003.
Values sent between devices are 32-bit elements; how exact they have to be, the bound alone decides.
A program may use at most 64 MiB of HBM per device.

v0:
```python
import math

import jax
import jax.numpy as jnp
from jax import lax
from jax.sharding import PartitionSpec as P

SOFT = 1.0


def pair_block(target_pos, target_str, target_mu, source_pos, source_str, source_mu, wavenumbers):
    freqs = wavenumbers.shape[0]
    offset = target_pos[:, None, :] - source_pos[:, :, None]
    squared = jnp.sum(offset * offset, axis=0) + SOFT
    inverse = lax.rsqrt(squared)
    distance = squared * inverse
    inverse_sq = inverse * inverse
    phase = wavenumbers[:, None, None] * distance[None]
    cosine = jnp.cos(phase)
    sine = jnp.sin(phase)
    deriv_real = -(cosine + phase * sine) * inverse_sq
    deriv_imag = (phase * cosine - sine) * inverse_sq
    tgt_real = target_str[:freqs, None, :]
    tgt_imag = target_str[freqs:, None, :]
    tmu_real = target_mu[:freqs, None, :]
    tmu_imag = target_mu[freqs:, None, :]
    src_real = source_str[:freqs, :, None]
    src_imag = source_str[freqs:, :, None]
    smu_real = source_mu[:freqs, :, None]
    smu_imag = source_mu[freqs:, :, None]
    prod_real = (
        tmu_real * src_real - tmu_imag * src_imag + smu_real * tgt_real - smu_imag * tgt_imag
    )
    prod_imag = (
        tmu_real * src_imag + tmu_imag * src_real + smu_real * tgt_imag + smu_imag * tgt_real
    )
    weight = jnp.sum(prod_real * deriv_real - prod_imag * deriv_imag, axis=0) * inverse
    return jnp.sum(weight[None] * offset, axis=1)


def pair_sweep(
    total, target_pos, target_str, target_mu, source_pos, source_str, source_mu, wavenumbers
):
    width = source_pos.shape[1]
    step = math.gcd(width, 32)

    def visit_block(carry, block_index):
        begin = block_index * step
        spos = lax.dynamic_slice_in_dim(source_pos, begin, step, 1)
        sstr = lax.dynamic_slice_in_dim(source_str, begin, step, 1)
        smu = lax.dynamic_slice_in_dim(source_mu, begin, step, 1)
        return (
            carry + pair_block(target_pos, target_str, target_mu, spos, sstr, smu, wavenumbers),
            None,
        )

    result, _ = lax.scan(visit_block, total, jnp.arange(width // step, dtype=jnp.int32))
    return result


def complex_times(left, right, freqs):
    left_real, left_imag = (left[:freqs], left[freqs:])
    right_real, right_imag = (right[:freqs], right[freqs:])
    return jnp.concatenate(
        [
            left_real * right_real - left_imag * right_imag,
            left_real * right_imag + left_imag * right_real,
        ],
        axis=0,
    )


def on_device(centroids, strengths, self_inv, wavenumbers, field_pos, targets, lists, connect):
    owned_count = centroids.shape[1]
    row_count = lax.axis_size("row")
    col_count = lax.axis_size("col")
    row_index = lax.axis_index("row")
    col_index = lax.axis_index("col")
    freqs = wavenumbers.shape[0]
    listed = lists.shape[1]
    panel_total = owned_count * row_count * col_count
    field_total = field_pos.shape[1] * row_count
    src_pos, src_str, src_inv = (
        lax.all_gather(centroids, "row", axis=1, tiled=True),
        lax.all_gather(strengths, "row", axis=1, tiled=True),
        lax.all_gather(self_inv, "row", axis=1, tiled=True),
    )
    source_count = src_pos.shape[1]
    panel_ids = lists.reshape(-1)
    owner_block = panel_ids // owned_count
    mask = (owner_block % col_count == col_index).astype(jnp.float32)
    local_ids = owner_block // col_count * owned_count + panel_ids % owned_count
    near = src_pos[:, local_ids]
    observer = jnp.repeat(field_pos, listed, axis=1)
    offset = observer - near
    distance = jnp.sqrt(jnp.sum(offset * offset, axis=0) + SOFT)
    inverse = mask / distance
    phase = wavenumbers[:, None] * distance[None]
    cosine = jnp.cos(phase)
    sine = jnp.sin(phase)
    near_str = src_str[:, local_ids]
    str_real = near_str[:freqs]
    str_imag = near_str[freqs:]
    part_real = (cosine * str_real - sine * str_imag) * inverse
    part_imag = (cosine * str_imag + sine * str_real) * inverse
    eta_part = jnp.concatenate(
        [
            part_real.reshape(freqs, -1, listed).sum(axis=2),
            part_imag.reshape(freqs, -1, listed).sum(axis=2),
        ],
        axis=0,
    )
    eta = lax.psum(eta_part, "col")
    resid = eta - targets
    misfit = lax.psum(jnp.sum(resid * resid), "row")
    objective = misfit / (freqs * field_total) + 1e-06
    rep_real = jnp.repeat(resid[:freqs], listed, axis=1)
    rep_imag = jnp.repeat(resid[freqs:], listed, axis=1)
    term_real = (cosine * rep_real + sine * rep_imag) * inverse
    term_imag = (cosine * rep_imag - sine * rep_real) * inverse
    terms = jnp.concatenate([term_real, term_imag], axis=0)
    source_part = jnp.zeros((2 * freqs, source_count), jnp.float32).at[:, local_ids].add(terms)
    source_part = source_part / objective
    late_scale = 1.0
    source_all = lax.psum(source_part, "row")
    mu_all = complex_times(source_all, src_inv, freqs)
    mu_own = lax.dynamic_slice_in_dim(mu_all, row_index * owned_count, owned_count, 1)
    tgt_pos, tgt_str, tgt_mu = (
        lax.all_gather(centroids, "col", axis=1, tiled=True),
        lax.all_gather(strengths, "col", axis=1, tiled=True),
        lax.all_gather(mu_own, "col", axis=1, tiled=True),
    )
    block_width = tgt_pos.shape[1]
    empty = jnp.zeros((3, block_width), jnp.float32)
    accum = pair_sweep(empty, tgt_pos, tgt_str, tgt_mu, src_pos, src_str, mu_all, wavenumbers)
    panel_sens = accum * (1.0 / math.sqrt(panel_total * freqs) * late_scale)
    vertex_local = connect - row_index * block_width
    vertex_part = jnp.zeros((3, block_width), jnp.float32)
    for corner in range(4):
        vertex_part = vertex_part.at[:, vertex_local[corner]].add(0.25 * panel_sens)
    vertex_own = lax.psum_scatter(vertex_part, "col", scatter_dimension=1, tiled=True)
    adjoint = mu_own * late_scale
    return (adjoint, vertex_own, objective)


def solution(mesh):
    return jax.shard_map(
        on_device,
        mesh=mesh,
        in_specs=(
            P(None, ("row", "col")),
            P(None, ("row", "col")),
            P(None, ("row", "col")),
            P(),
            P(None, "row"),
            P(None, "row"),
            P("row", None),
            P(None, "row"),
        ),
        out_specs=(P(None, ("row", "col")), P(None, ("row", "col")), P()),
        check_vma=False,
    )
```

profile of v0, /device:TPU:0, one launch (start us, length us, event | category | flops | bytes accessed | tf_op | source)
XLA Modules:
  0.0 445.4 jit_solution(7909612287266478152)
XLA Ops:
  9.2 15.7 %all_gather.19 = f32[32,256]{0,1:T(8,128)S(1)} all-gather(f32[32,32]{0,1:T(8,128)S(1)} %copy.150), channel_id=1, replica_groups=mesh['row'=8,'col'=4] {'row'}, dimensions={1}, use_global_device_ids=true | all-gather | bytes 36864 | tf_op jit(solution)/shard_map/all_gather | solution.py:85
  24.9 8.2 %all_gather.22 = f32[32,128]{0,1:T(8,128)S(1)} all-gather(f32[32,32]{0,1:T(8,128)S(1)} %copy.150), channel_id=1, replica_groups=mesh['row'=8,'col'=4] {'col'}, dimensions={1}, use_global_device_ids=true | all-gather | bytes 20480 | tf_op jit(solution)/shard_map/all_gather | solution.py:130
  33.1 12.8 %all-gather = f32[8,32,3]{1,2,0:T(4,128)S(1)} all-gather(f32[1,32,3]{1,2,0:T(4,128)} %bitcast.52), channel_id=1, replica_groups=mesh['row'=8,'col'=4] {'row'}, dimensions={0}, use_global_device_ids=true | all-gather | bytes 3456 | tf_op jit(solution)/shard_map/all_gather | solution.py:84
  45.9 8.0 %all-gather.1 = f32[4,32,3]{1,2,0:T(4,128)S(1)} all-gather(f32[1,32,3]{1,2,0:T(4,128)} %bitcast.53), channel_id=1, replica_groups=mesh['row'=8,'col'=4] {'col'}, dimensions={0}, use_global_device_ids=true | all-gather | bytes 1920 | tf_op jit(solution)/shard_map/all_gather | solution.py:129
  55.0 54.4 %gather_fusion = f32[16384,3]{1,0:T(8,128)} fusion(f32[3,256]{0,1:T(8,128)S(1)} %bitcast.47, s32[16384]{0:T(1024)S(1)} %broadcast_clamp_fusion), kind=kCustom, calls=%fused_computation | custom fusion | bytes 458752 | tf_op jit(solution)/shard_map/gather | solution.py:93
  110.3 54.4 %gather_fusion.1 = f32[16384,32]{1,0:T(8,128)} fusion(f32[32,256]{0,1:T(8,128)S(1)} %all_gather.19, s32[16384]{0:T(1024)S(1)} %broadcast_clamp_fusion), kind=kCustom, calls=%fused_computation.1 | custom fusion | bytes 4259840 | tf_op jit(solution)/shard_map/gather | solution.py:101
  164.6 5.1 %copy.151 = f32[16384,32]{0,1:T(8,128)S(1)} copy(f32[16384,32]{1,0:T(8,128)} %gather_fusion.1) | data formatting | bytes 4194304 | tf_op jit(solution)/shard_map/gather | solution.py:101
  169.8 4.6 %fusion.12 = f32[16384]{0:T(1024)S(1)} fusion(f32[16384,3]{1,0:T(8,128)} %gather_fusion, f32[3,256]{0,1:T(8,128)S(1)} %copy.148), kind=kLoop, calls=%fused_computation.35 | loop fusion | flops 131072 | bytes 265216 | tf_op jit(solution)/shard_map/reduce_sum | solution.py:96
  174.5 5.0 %fusion.22 = (f32[16,16384]{1,0:T(8,128)}, f32[16,16384]{1,0:T(8,128)S(1)}) fusion(f32[32,16384]{1,0:T(8,128)S(1)} %bitcast.48, f32[16384]{0:T(1024)S(1)} %get-tuple-element.223, f32[16384]{0:T(1024)S(1)} %get-tuple-element.222, f32[16]{0:T(128)S(1)} %copy-done.3), kind=kLoop, calls=%fused_computation.48 | loop fusion | flops 2359296 | bytes 4325440 | tf_op jit(solution)/shard_map/mul | solution.py:104
  179.5 5.9 %copy.172 = f32[16,16384]{0,1:T(8,128)} copy(f32[16,16384]{1,0:T(8,128)} %get-tuple-element.218) | data formatting | bytes 2097152 | tf_op jit(solution)/shard_map/reshape | solution.py:108
  185.4 5.0 %bitcast_reduce_fusion.1 = f32[16,256]{0,1:T(8,128)S(1)} fusion(f32[16,16384]{0,1:T(8,128)} %copy.172), kind=kLoop, calls=%fused_computation.32 | loop fusion | flops 258048 | bytes 1064960 | tf_op jit(solution)/shard_map/reduce_sum | solution.py:108
  190.6 4.6 %copy.173 = f32[16,16384]{0,1:T(8,128)} copy(f32[16,16384]{1,0:T(8,128)S(1)} %get-tuple-element.219) | data formatting | bytes 2097152 | tf_op jit(solution)/shard_map/reshape | solution.py:109
  195.2 5.0 %bitcast_reduce_fusion = f32[16,256]{0,1:T(8,128)S(1)} fusion(f32[16,16384]{0,1:T(8,128)} %copy.173), kind=kLoop, calls=%fused_computation.31 | loop fusion | flops 258048 | bytes 1064960 | tf_op jit(solution)/shard_map/reduce_sum | solution.py:109
  200.3 15.3 %psum.21 = f32[32,256]{1,0:T(8,128)S(1)} all-reduce(f32[32,256]{1,0:T(8,128)S(1)} %pad_maximum_fusion.1), channel_id=1, replica_groups=mesh['row'=8,'col'=4] {'col'}, use_global_device_ids=true, to_apply=%region_3.4 | all-reduce | flops 8192 | bytes 65536 | tf_op jit(solution)/shard_map/psum | solution.py:113
  219.4 1.6 reshape.387
  221.1 5.2 %fusion.26 = (f32[16,16384]{1,0:T(8,128)S(1)}, f32[16,16384]{1,0:T(8,128)S(1)}) fusion(f32[16,16384]{1,0:T(8,128)} %reshape.387, f32[16,16384]{1,0:T(8,128)S(1)} %reshape.386, f32[16384]{0:T(1024)S(1)} %get-tuple-element.223, f32[16384]{0:T(1024)S(1)} %get-tuple-element.222, f32[16]{0:T(128)} %param.13), kind=kLoop, calls=%fused_computation.52 | loop fusion | flops 2359296 | bytes 4325440 | tf_op jit(solution)/shard_map/mul | solution.py:119
  226.5 4.7 %copy.157 = f32[16384,32]{1,0:T(8,128)} copy(f32[16384,32]{0,1:T(8,128)S(1)} %maximum_bitcast_fusion) | data formatting | bytes 4194304 | tf_op jit(solution)/shard_map/concatenate | solution.py:121
  231.2 14.2 %psum.22 = f32[]{:T(128)} all-reduce(f32[]{:T(128)} %get-tuple-element.200), channel_id=1, replica_groups=mesh['row'=8,'col'=4] {'row'}, use_global_device_ids=true, to_apply=%region_6.7 | all-reduce | flops 1 | bytes 8 | tf_op jit(solution)/shard_map/psum | solution.py:115
  245.4 87.7 %scatter_custom_fusion = f32[32,256]{0,1:T(8,128)S(1)} fusion(s32[16384]{0:T(1024)S(1)} %bitcast.50, f32[16384,32]{1,0:T(8,128)} %copy.157, f32[]{:T(128)} %constant.79.clone.1), kind=kCustom, calls=%fused_computation.84 | custom fusion | flops 524288 | bytes 33280 | tf_op jit(solution)/shard_map/scatter-add | solution.py:122
  333.7 27.2 %psum.23 = f32[32,256]{0,1:T(8,128)S(1)} all-reduce(f32[32,256]{0,1:T(8,128)S(1)} %broadcast_divide_fusion), channel_id=1, replica_groups=mesh['row'=8,'col'=4] {'row'}, use_global_device_ids=true, to_apply=%region_7.8 | all-reduce | flops 8192 | bytes 65536 | tf_op jit(solution)/shard_map/psum | solution.py:125
  360.9 14.0 %all_gather.20 = f32[32,256]{0,1:T(8,128)S(1)} all-gather(f32[32,32]{0,1:T(8,128)S(1)} %copy.158), channel_id=1, replica_groups=mesh['row'=8,'col'=4] {'row'}, dimensions={1}, use_global_device_ids=true | all-gather | bytes 36864 | tf_op jit(solution)/shard_map/all_gather | solution.py:86
  375.2 7.4 %all_gather.21 = f32[32,128]{0,1:T(8,128)S(1)} all-gather(f32[32,32]{0,1:T(8,128)S(1)} %fusion.38), channel_id=1, replica_groups=mesh['row'=8,'col'=4] {'col'}, dimensions={1}, use_global_device_ids=true | all-gather | bytes 20480 | tf_op jit(solution)/shard_map/all_gather | solution.py:131
  382.8 26.3 %while.11 = (s32[]{:T(128)}, f32[3,128]{1,0:T(4,128)S(1)}, f32[32,128]{1,0:T(8,128)S(1)}, s32[8]{0:T(128)S(1)}, f32[32,256]{0,1:T(8,128)S(1)}, /*index=5*/f32[32...) while((s32[]{:T(128)}, f32[3,128]{1,0:T(4,128)S(1)}, ...), condition=%wide.region_12.13_spmd.clone, body=%wide.region_8.12_spmd.clone.sunk | while | flops 1790344 | bytes 330537 | solution.py:57
  384.6 1.4 fusion.52
  387.9 1.4 fusion.52
  391.2 1.4 fusion.52
  394.5 1.4 fusion.52
  397.8 1.4 fusion.52
  401.1 1.4 fusion.52
  407.7 1.4 fusion.52
  415.6 20.4 %reduce-scatter.2.cloned.1.call-done = f32[3,32]{0,1:T(8,128)} async-done(((f32[3,128]{0,1:T(8,128)}), f32[3,32]{0,1:T(8,128)}) %reduce-scatter.2.cloned.1.call-update) | async-done | bytes 400 | tf_op jit(solution)/shard_map/reduce_scatter | solution.py:141
  436.0 1.4 copy.171
  (158 shorter events, 26.1 us)
Async XLA Ops:
  7.2 428.9 %reduce-scatter.2.cloned.1.call-start = ((), (), s32[]{:S(2)}) async-start(), calls=%async_computation.1 | async-start | bytes 81920 | tf_op jit(solution)/shard_map/reduce_scatter | solution.py:141
  169.8 4.8 %copy-start.3 = (f32[16]{0:T(128)S(1)}, f32[16]{0:T(128)}, u32[]{:S(2)}) copy-start(f32[16]{0:T(128)} %param.13) | copy-start | bytes 196
  190.6 25.1 %copy-start.1 = (f32[32,256]{1,0:T(8,128)S(1)}, f32[32,256]{1,0:T(8,128)}, u32[]{:S(2)}) copy-start(f32[32,256]{1,0:T(8,128)} %param.15) | copy-start | bytes 98308
  226.3 134.6 %copy-start.2 = (f32[32,32]{1,0:T(8,128)S(1)}, f32[32,32]{1,0:T(8,128)}, u32[]{:S(2)}) copy-start(f32[32,32]{1,0:T(8,128)} %param.12) | copy-start | bytes 12292
  226.3 156.5 %copy-start.4 = (f32[16]{0:T(128)S(1)}, f32[16]{0:T(128)}, u32[]{:S(2)}) copy-start(f32[16]{0:T(128)} %param.13) | copy-start | bytes 196
  226.5 182.8 %copy-start.5 = (s32[4,128]{1,0:T(4,128)S(1)}, s32[4,128]{1,0:T(4,128)}, u32[]{:S(2)}) copy-start(s32[4,128]{1,0:T(4,128)} %param.17) | copy-start | bytes 6148
  414.3 0.6 copy-start
Sparse Core Ops, SparseCore 0:
  415.1 20.9 reduce-scatter.1
where the time goes:
time: 446 us; the launch traced here: 445 us
  local copies, waits for them, and re-layouts  148 us (33%)
  other arithmetic  132 us (30%)
  blocking collectives  123 us (28%)
  waiting for transfers between devices  20.4 us (5%)
  between operations  16.1 us (4%)
  loops' own time  5.67 us (1%)
    scatter-add x1, other arithmetic, on_device(): jnp.zeros((2 * freqs, source_count), jnp.float32).at[:, local_ids]  87.7 us
    gather x2, local copies, waits for them, and re-layouts, on_device(): near_str = src_str[:, local_ids]  59.5 us
    gather x1, local copies, waits for them, and re-layouts, on_device(): near = src_pos[:, local_ids]  54.4 us
    psum x1, blocking collectives, on_device(): source_all = lax.psum(source_part, 'row')  27.2 us
    reduce_scatter x1, waiting for transfers between devices, on_device(): lax.psum_scatter(vertex_part, 'col', scatter_dimension=1, tiled=True)  20.4 us
    all_gather x1, blocking collectives, on_device(): lax.all_gather(strengths, 'row', axis=1, tiled=True)  15.7 us
    psum x1, blocking collectives, on_device(): eta = lax.psum(eta_part, 'col')  15.3 us
    psum x1, blocking collectives, on_device(): misfit = lax.psum(jnp.sum(resid * resid), 'row')  14.2 us
  transfers between devices with their start and end apart: 1, of which 1 were waited for; matrix products, arithmetic and copies ran while one was open for 0% of the time, Pallas kernels for 0%

commit v1 on v0

v1 whole, which is shorter than its diff:
```python
import functools
import math

import jax
import jax.numpy as jnp
from jax import lax
from jax.experimental import pallas as pl
from jax.experimental.pallas import tpu as pltpu
from jax.sharding import PartitionSpec as P

SOFT = 1.0
LANES = 128
STEP = 16
MESH = pl.DeviceIdType.MESH
SIN_COEF = (6.283182818550509, -41.34142139863338, 81.59618387150631, -76.58010050947591, 41.205394790207706, -12.27126223106381)
COS_COEF = (0.999999221570582, -19.73898251610168, 64.92872660897218, -85.2723968955171, 58.7940381912709, -21.076781284621926)
MAGIC = 12582912.0


def horner(coefs, x):
    total = jnp.full_like(x, coefs[-1])
    for coef in coefs[-2::-1]:
        total = total * x + coef
    return total


def sincos_turns(turns):
    part = turns - ((turns + MAGIC) - MAGIC)
    square = part * part
    return part * horner(SIN_COEF, square), horner(COS_COEF, square)


def kernel(
    dims,
    cen_ref,
    str_ref,
    inv_ref,
    wave_ref,
    field_ref,
    targ_ref,
    lists_ref,
    conn_ref,
    adj_out,
    vert_out,
    obj_out,
    square_buf,
    src_buf,
    tgt_buf,
    src_rows,
    list_buf,
    list_rows,
    count_buf,
    green_cos,
    green_sin,
    eta_acc,
    eta_buf,
    resid_buf,
    send_source,
    recv_source,
    mu_src,
    mu_tgt,
    mu_rows,
    deriv_re,
    deriv_im,
    sens_buf,
    vert_send,
    vert_recv,
    send_row,
    recv_row,
    send_col,
    recv_col,
):
    rows, cols, own, freqs, points, listed, keep = dims
    sources, targets = rows * own, cols * own
    pos_at, inv_at = 2 * freqs, 2 * freqs + 8
    row, col = lax.axis_index("row"), lax.axis_index("col")

    def row_peer(k):
        return (lax.rem(row + k, rows), col)

    def col_peer(k):
        return (row, lax.rem(col + k, cols))

    barrier = pltpu.get_barrier_semaphore()
    for k in range(1, rows):
        pl.semaphore_signal(barrier, inc=1, device_id=row_peer(k), device_id_type=MESH)
    for k in range(1, cols):
        pl.semaphore_signal(barrier, inc=1, device_id=col_peer(k), device_id_type=MESH)

    own_src = pl.ds(pl.multiple_of(row * own, own), own)
    own_tgt = pl.ds(pl.multiple_of(col * own, own), own)

    square_buf[...] = jnp.zeros_like(square_buf)
    square_buf[0 : 2 * freqs, 0:own] = str_ref[...]
    square_buf[pos_at : pos_at + 3, 0:own] = cen_ref[...]
    square_buf[inv_at : inv_at + 2 * freqs, 0:own] = inv_ref[...]
    mine = jnp.transpose(square_buf[...])[0:own, :]
    src_buf[own_src, :] = mine
    tgt_buf[own_tgt, :] = mine

    def push(stage, source, target, peer, sems, k):
        copy = pltpu.make_async_remote_copy(
            src_ref=source,
            dst_ref=target,
            send_sem=sems[0].at[stage, k],
            recv_sem=sems[1].at[stage, k],
            device_id=peer,
            device_id_type=MESH,
        )
        copy.start()
        return copy

    row_sems, col_sems = (send_row, recv_row), (send_col, recv_col)
    pl.semaphore_wait(barrier, rows + cols - 2)
    done = []
    first = [
        push(0, src_buf.at[own_src], src_buf.at[own_src], row_peer(k), row_sems, k)
        for k in range(1, rows)
    ]
    side = [
        push(0, tgt_buf.at[own_tgt], tgt_buf.at[own_tgt], col_peer(k), col_sems, k)
        for k in range(1, cols)
    ]

    list_buf[...] = jnp.zeros_like(list_buf)
    list_buf[:, 0:listed] = lists_ref[...].astype(jnp.float32)
    list_rows[...] = jnp.transpose(list_buf[...])

    def count_step(block, carry):
        start = pl.multiple_of(block * own, own)
        ids = lax.broadcasted_iota(jnp.int32, (own, points), 0) + (block * cols + col) * own
        ids = ids.astype(jnp.float32)
        total = jnp.zeros((own, points), jnp.float32)
        for entry in range(listed):
            total = total + jnp.where(list_rows[entry : entry + 1, :] == ids, 1.0, 0.0)
        count_buf[pl.ds(start, own), :] = total
        return carry

    lax.fori_loop(0, rows, count_step, 0)
    eta_acc[...] = jnp.zeros_like(eta_acc)
    field = [field_ref[axis : axis + 1, :] for axis in range(3)]
    waves = [wave_ref[f] for f in range(freqs)]
    turns = [wave * (0.5 / math.pi) for wave in waves]

    for copy in first:
        copy.wait_recv()

    def field_step(step, carry):
        span = pl.ds(pl.multiple_of(step * STEP, STEP), STEP)
        block = src_buf[span, :]
        squared = SOFT
        for axis in range(3):
            gap = field[axis] - block[:, pos_at + axis : pos_at + axis + 1]
            squared = gap * gap + squared
        inverse = lax.rsqrt(squared)
        distance = squared * inverse
        gain = count_buf[span, :] * inverse
        for f in range(freqs):
            sine, cosine = sincos_turns(distance * turns[f])
            cosine, sine = cosine * gain, sine * gain
            green_cos[f, span, :] = cosine
            green_sin[f, span, :] = sine
            real, imag = block[:, f : f + 1], block[:, freqs + f : freqs + f + 1]
            part_real = cosine * real - sine * imag
            part_imag = cosine * imag + sine * real
            eta_acc[f] += jnp.sum(part_real.reshape(STEP // 8, 8, points), axis=0)
            eta_acc[freqs + f] += jnp.sum(part_imag.reshape(STEP // 8, 8, points), axis=0)
        return carry

    lax.fori_loop(0, sources // STEP, field_step, 0)
    eta_buf[col] = jnp.sum(eta_acc[...], axis=1)
    eta_copies = [
        push(1, eta_buf.at[col], eta_buf.at[col], col_peer(k), col_sems, k)
        for k in range(1, cols)
    ]

    for copy in side:
        copy.wait_recv()
    src_rows[...] = jnp.transpose(src_buf[...])
    place = [src_rows[pos_at + axis : pos_at + axis + 1, :] for axis in range(3)]

    def gaps(block):
        return [block[:, pos_at + axis : pos_at + axis + 1] - place[axis] for axis in range(3)]

    def lengths(offset):
        squared = offset[0] * offset[0] + offset[1] * offset[1] + offset[2] * offset[2] + SOFT
        inverse = lax.rsqrt(squared)
        return squared * inverse, inverse

    def derivative(f, distance, inverse_sq):
        phase = distance * waves[f]
        sine, cosine = sincos_turns(distance * turns[f])
        return -(cosine + phase * sine) * inverse_sq, (phase * cosine - sine) * inverse_sq

    if keep:

        def deriv_step(step, carry):
            span = pl.ds(pl.multiple_of(step * STEP, STEP), STEP)
            distance, inverse = lengths(gaps(tgt_buf[span, :]))
            for f in range(freqs):
                real, imag = derivative(f, distance, inverse * inverse)
                deriv_re[f, span, :] = real
                deriv_im[f, span, :] = imag
            return carry

        lax.fori_loop(0, targets // STEP, deriv_step, 0)

    for copy in eta_copies:
        copy.wait_recv()
    eta = eta_buf[0]
    for k in range(1, cols):
        eta = eta + eta_buf[k]
    resid = eta - targ_ref[...]
    resid_buf[...] = resid
    misfit = jnp.sum(jnp.sum(resid * resid, axis=0, keepdims=True), axis=1, keepdims=True)
    lane = lax.broadcasted_iota(jnp.int32, (STEP, LANES), 1)

    def source_step(step, carry):
        span = pl.ds(pl.multiple_of(step * STEP, STEP), STEP)
        total = jnp.where(lane == 2 * freqs, misfit, 0.0)
        for f in range(freqs):
            cosine, sine = green_cos[f, span, :], green_sin[f, span, :]
            real = resid_buf[f : f + 1, :]
            imag = resid_buf[freqs + f : freqs + f + 1, :]
            sum_real = jnp.sum(cosine * real + sine * imag, axis=1, keepdims=True)
            sum_imag = jnp.sum(cosine * imag - sine * real, axis=1, keepdims=True)
            total = jnp.where(lane == f, sum_real, total)
            total = jnp.where(lane == freqs + f, sum_imag, total)
        send_source[span, :] = total
        return carry

    lax.fori_loop(0, sources // STEP, source_step, 0)
    source_copies = []
    for k in range(1, rows):
        there = pl.ds(pl.multiple_of(lax.rem(row + k, rows) * own, own), own)
        source_copies.append(
            push(1, send_source.at[there], recv_source.at[own_src], row_peer(k), row_sems, k)
        )
    recv_source[own_src, :] = send_source[own_src, :]
    base = row * targets
    vertex = lax.broadcasted_iota(jnp.int32, (targets, targets), 0) + base
    share = jnp.zeros((targets, targets), jnp.float32)
    for corner in range(4):
        share = share + jnp.where(conn_ref[corner : corner + 1, :] == vertex, 0.25, 0.0)
    for copy in source_copies:
        copy.wait_recv()
    source = recv_source[0:own, :]
    for r in range(1, rows):
        source = source + recv_source[r * own : (r + 1) * own, :]
    objective = source[:, 2 * freqs : 2 * freqs + 1] / (freqs * points * rows) + 1e-06
    obj_out[...] = objective[0:1, :]
    source = source / objective
    lane = lax.broadcasted_iota(jnp.int32, (own, LANES), 1)
    low = lane < freqs
    inv_own = pltpu.roll(mine, LANES - inv_at, 1)
    inv_turn = jnp.where(low, -pltpu.roll(inv_own, LANES - freqs, 1), pltpu.roll(inv_own, freqs, 1))
    real = jnp.where(low, source, pltpu.roll(source, freqs, 1))
    imag = jnp.where(low, pltpu.roll(source, LANES - freqs, 1), source)
    mu = jnp.where(lane < 2 * freqs, real * inv_own + imag * inv_turn, 0.0)
    mu_src[own_src, :] = mu
    mu_tgt[own_tgt, :] = mu
    mu_copies = [
        push(2, mu_src.at[own_src], mu_src.at[own_src], row_peer(k), row_sems, k)
        for k in range(1, rows)
    ] + [
        push(2, mu_tgt.at[own_tgt], mu_tgt.at[own_tgt], col_peer(k), col_sems, k)
        for k in range(1, cols)
    ]
    square_buf[0:own, :] = mu
    adj_out[...] = jnp.transpose(square_buf[...])[0 : 2 * freqs, 0:own]
    for copy in mu_copies:
        copy.wait_recv()
    mu_rows[...] = jnp.transpose(mu_src[...])
    scale = 1.0 / math.sqrt(sources * cols * freqs)
    lane = lax.broadcasted_iota(jnp.int32, (STEP, LANES), 1)

    def sens_step(step, carry):
        span = pl.ds(pl.multiple_of(step * STEP, STEP), STEP)
        block, tmu = tgt_buf[span, :], mu_tgt[span, :]
        offset = gaps(block)
        distance, inverse = lengths(offset)
        weight = jnp.zeros((STEP, sources), jnp.float32)
        for f in range(freqs):
            g = freqs + f
            if keep:
                der_real, der_imag = deriv_re[f, span, :], deriv_im[f, span, :]
            else:
                der_real, der_imag = derivative(f, distance, inverse * inverse)
            t_real, t_imag = block[:, f : f + 1], block[:, g : g + 1]
            tm_real, tm_imag = tmu[:, f : f + 1], tmu[:, g : g + 1]
            s_real, s_imag = src_rows[f : f + 1, :], src_rows[g : g + 1, :]
            sm_real, sm_imag = mu_rows[f : f + 1, :], mu_rows[g : g + 1, :]
            prod_real = tm_real * s_real - tm_imag * s_imag + sm_real * t_real - sm_imag * t_imag
            prod_imag = tm_real * s_imag + tm_imag * s_real + sm_real * t_imag + sm_imag * t_real
            weight = weight + (prod_real * der_real - prod_imag * der_imag)
        weight = weight * inverse
        total = jnp.zeros((STEP, LANES), jnp.float32)
        for axis in range(3):
            part = jnp.sum(weight * offset[axis], axis=1, keepdims=True)
            total = jnp.where(lane == axis, part * scale, total)
        sens_buf[span, :] = total
        return carry

    lax.fori_loop(0, targets // STEP, sens_step, 0)
    vert_send[...] = jnp.dot(
        share,
        sens_buf[...],
        preferred_element_type=jnp.float32,
        precision=lax.Precision.HIGHEST,
    )
    vert_copies = []
    for k in range(1, cols):
        there = pl.ds(pl.multiple_of(lax.rem(col + k, cols) * own, own), own)
        vert_copies.append(
            push(3, vert_send.at[there], vert_recv.at[own_tgt], col_peer(k), col_sems, k)
        )
    vert_recv[own_tgt, :] = vert_send[own_tgt, :]
    for copy in vert_copies:
        copy.wait_recv()
    total = vert_recv[0:own, :]
    for k in range(1, cols):
        total = total + vert_recv[k * own : (k + 1) * own, :]
    square_buf[0:own, :] = total
    vert_out[...] = jnp.transpose(square_buf[...])[0:3, 0:own]
    for copy in first + side + eta_copies + source_copies + mu_copies + vert_copies:
        copy.wait_send()


def on_device(centroids, strengths, self_inv, wavenumbers, field_pos, targets, lists, connect):
    own = centroids.shape[1]
    rows, cols = lax.axis_size("row"), lax.axis_size("col")
    freqs = wavenumbers.shape[0]
    points, listed = lists.shape
    sources, block = rows * own, cols * own
    keep = freqs * block * sources * 8 <= 16 * 2**20
    kept = (freqs, block, sources) if keep else (1, 8, LANES)
    f32 = jnp.float32
    vmem = pl.BlockSpec(memory_space=pltpu.VMEM)
    smem = pl.BlockSpec(memory_space=pltpu.SMEM)
    adjoint, vertex, objective = pl.pallas_call(
        functools.partial(kernel, (rows, cols, own, freqs, points, listed, keep)),
        out_shape=(
            jax.ShapeDtypeStruct((2 * freqs, own), f32),
            jax.ShapeDtypeStruct((3, own), f32),
            jax.ShapeDtypeStruct((1, 1), f32),
        ),
        in_specs=[vmem, vmem, vmem, smem, vmem, vmem, vmem, vmem],
        out_specs=(vmem, vmem, vmem),
        scratch_shapes=[
            pltpu.VMEM((LANES, LANES), f32),
            pltpu.VMEM((sources, LANES), f32),
            pltpu.VMEM((block, LANES), f32),
            pltpu.VMEM((LANES, sources), f32),
            pltpu.VMEM((points, LANES), f32),
            pltpu.VMEM((LANES, points), f32),
            pltpu.VMEM((sources, points), f32),
            pltpu.VMEM((freqs, sources, points), f32),
            pltpu.VMEM((freqs, sources, points), f32),
            pltpu.VMEM((2 * freqs, 8, points), f32),
            pltpu.VMEM((cols, 2 * freqs, points), f32),
            pltpu.VMEM((2 * freqs, points), f32),
            pltpu.VMEM((sources, LANES), f32),
            pltpu.VMEM((sources, LANES), f32),
            pltpu.VMEM((sources, LANES), f32),
            pltpu.VMEM((block, LANES), f32),
            pltpu.VMEM((LANES, sources), f32),
            pltpu.VMEM(kept, f32),
            pltpu.VMEM(kept, f32),
            pltpu.VMEM((block, LANES), f32),
            pltpu.VMEM((block, LANES), f32),
            pltpu.VMEM((block, LANES), f32),
            pltpu.SemaphoreType.DMA((3, rows)),
            pltpu.SemaphoreType.DMA((3, rows)),
            pltpu.SemaphoreType.DMA((4, cols)),
            pltpu.SemaphoreType.DMA((4, cols)),
        ],
        compiler_params=pltpu.CompilerParams(
            collective_id=0, has_side_effects=True, vmem_limit_bytes=52 * 2**20
        ),
    )(centroids, strengths, self_inv, wavenumbers, field_pos, targets, lists, connect)
    return adjoint, vertex, objective.reshape(())


def solution(mesh):
    return jax.shard_map(
        on_device,
        mesh=mesh,
        in_specs=(
            P(None, ("row", "col")),
            P(None, ("row", "col")),
            P(None, ("row", "col")),
            P(),
            P(None, "row"),
            P(None, "row"),
            P("row", None),
            P(None, "row"),
        ),
        out_specs=(P(None, ("row", "col")), P(None, ("row", "col")), P()),
        check_vma=False,
    )
```

time: 446 us -> 44.7 us (0.10)
  local copies, waits for them, and re-layouts: 148 us -> 2.19 us
  other arithmetic: 132 us -> 0 us
  blocking collectives: 123 us -> 0 us
  Pallas kernels: 0 us -> 39.9 us
  waiting for transfers between devices: 20.4 us -> 0 us
  between operations: 16.1 us -> 2.45 us
  loops' own time: 5.67 us -> 0 us
    gather x3 -> x0, local copies, waits for them, and re-layouts: 114 us -> none  [the longest x2 59.5 us: on_device(): near_str = src_str[:, local_ids]]
    scatter-add x5 -> x0, other arithmetic: 92.6 us -> none  [the longest x1 87.7 us: on_device(): jnp.zeros((2 * freqs, source_count), jnp.float32).at[:, local_ids]]
    all_gather x6 -> x0, blocking collectives: 66.1 us -> none  [the longest x1 15.7 us: on_device(): lax.all_gather(strengths, 'row', axis=1, tiled=True)]
    psum x3 -> x0, blocking collectives: 56.7 us -> none  [the longest x1 27.2 us: on_device(): source_all = lax.psum(source_part, 'row')]
    pallas_call x0 -> x1, Pallas kernels: none -> 39.9 us  [on_device(): pl.pallas_call(functools.partial(kernel, (rows, cols, own, freqs, points,...]
    reduce_sum x28 -> x0, other arithmetic: 27.6 us -> none  [the longest x8 10.9 us: pair_block(): jnp.sum(prod_real * deriv_real - prod_imag * deriv_imag, axis=0) * inverse]
    reduce_scatter x1 -> x0, waiting for transfers between devices: 20.4 us -> none  [on_device(): lax.psum_scatter(vertex_part, 'col', scatter_dimension=1, tiled=True)]
    reshape x6 -> x0, local copies, waits for them, and re-layouts: 13.1 us -> none  [the longest x1 5.95 us: on_device(): part_real.reshape(freqs, -1, listed).sum(axis=2)]
  transfers between devices with their start and end apart: 1 -> 0, of which waited for: 1 -> 0; matrix products, arithmetic and copies ran while one was open for 0% -> 0% of each run, Pallas kernels for 0% -> 0%
where the time goes in v1:
time: 44.7 us; the launch traced here: 44.5 us
  Pallas kernels  39.9 us (89%)
  between operations  2.45 us (5%)
  local copies, waits for them, and re-layouts  2.19 us (5%)
    pallas_call x1, Pallas kernels, on_device(): pl.pallas_call(functools.partial(kernel, (rows, cols, own, freqs, points,...  39.9 us
    unnamed x17, local copies, waits for them, and re-layouts  2.19 us

profile of v1, /device:TPU:0, one launch (start us, length us, event | category | flops | bytes accessed | tf_op | source)
XLA Modules:
  0.0 44.5 jit_solution(11794059059101750328)
XLA Ops:
  0.6 0.0 copy-start.5
  0.6 0.0 copy-start
  0.7 0.0 copy-start.3
  0.7 0.0 copy-start.6
  0.7 0.0 copy-start.2
  0.7 0.0 copy-start.1
  0.7 0.0 copy-start.4
  0.7 1.0 %copy.11.lists_ref = s32[256,64]{1,0:T(8,128)S(1)} copy(s32[256,64]{0,1:T(8,128)} %param.14) | data formatting | bytes 131072 | tf_op args[6]
  1.7 0.0 copy-done.5
  1.7 0.0 copy-done
  1.7 0.0 copy-done.3
  1.7 0.0 copy-done.6
  1.7 0.0 copy-done.2
  1.7 0.0 copy-done.1
  1.7 0.0 copy-done.4
  1.7 39.9 %shard_map.103 = (f32[32,32]{1,0:T(8,128)S(1)}, f32[3,32]{1,0:T(4,128)S(1)}, f32[1,1]{1,0:T(1,128)}) custom-call(f32[3,32]{1,0:T(4,128)S(1)} %copy-done.4, f32[32,32]{1,0:T(8,128)S(1)} %copy-done.1, f32[32,32]{1,0:T(8,128)S(1)} %copy-done.2, f32[16]{0:T(128)S(1)} %copy-done.6, f32[3,256]{1,0:T(4,128)S(1)} %copy-done.3, f32[32,256]{1,0:T(8,128)S(1)} %copy-done, ...), custom_call_target="tpu_custom_call" | custom-call | tf_op jit(solution)/shard_map/pallas_call | solution.py:340
  41.6 0.6 %copy.15 = f32[32,32]{1,0:T(8,128)} copy(f32[32,32]{1,0:T(8,128)S(1)} %get-tuple-element.12) | data formatting | bytes 8192
  42.2 0.6 %copy.16 = f32[3,32]{1,0:T(4,128)} copy(f32[3,32]{1,0:T(4,128)S(1)} %get-tuple-element.13) | data formatting | bytes 768
Async XLA Ops:
  0.6 1.0 %copy-start.5 = (s32[4,128]{1,0:T(4,128)S(1)}, s32[4,128]{1,0:T(4,128)}, u32[]{:S(2)}) copy-start(s32[4,128]{1,0:T(4,128)} %conn_ref.1) | copy-start | bytes 6148
  0.6 1.0 %copy-start = (f32[32,256]{1,0:T(8,128)S(1)}, f32[32,256]{1,0:T(8,128)}, u32[]{:S(2)}) copy-start(f32[32,256]{1,0:T(8,128)} %targ_ref.1) | copy-start | bytes 98308
  0.7 1.0 %copy-start.3 = (f32[3,256]{1,0:T(4,128)S(1)}, f32[3,256]{1,0:T(4,128)}, u32[]{:S(2)}) copy-start(f32[3,256]{1,0:T(4,128)} %field_ref.1) | copy-start | bytes 9220
  0.7 1.0 %copy-start.6 = (f32[16]{0:T(128)S(1)}, f32[16]{0:T(128)}, u32[]{:S(2)}) copy-start(f32[16]{0:T(128)} %wave_ref.1) | copy-start | bytes 196
  0.7 1.0 %copy-start.2 = (f32[32,32]{1,0:T(8,128)S(1)}, f32[32,32]{1,0:T(8,128)}, u32[]{:S(2)}) copy-start(f32[32,32]{1,0:T(8,128)} %inv_ref.1) | copy-start | bytes 12292
  0.7 1.0 %copy-start.1 = (f32[32,32]{1,0:T(8,128)S(1)}, f32[32,32]{1,0:T(8,128)}, u32[]{:S(2)}) copy-start(f32[32,32]{1,0:T(8,128)} %str_ref.1) | copy-start | bytes 12292
  0.7 1.0 %copy-start.4 = (f32[3,32]{1,0:T(4,128)S(1)}, f32[3,32]{1,0:T(4,128)}, u32[]{:S(2)}) copy-start(f32[3,32]{1,0:T(4,128)} %cen_ref.1) | copy-start | bytes 1156

commit v2 on v1

--- a/solution.py
+++ b/solution.py
@@ -44,10 +44,11 @@
     vert_out,
     obj_out,
     square_buf,
+    src_pack,
+    tgt_pack,
     src_buf,
     tgt_buf,
     src_rows,
-    list_buf,
     list_rows,
     count_buf,
     green_cos,
@@ -57,11 +58,15 @@
     resid_buf,
     send_source,
     recv_source,
+    mu_src_pack,
+    mu_tgt_pack,
     mu_src,
     mu_tgt,
     mu_rows,
     deriv_re,
     deriv_im,
+    turned_re,
+    turned_im,
     sens_buf,
     vert_send,
     vert_recv,
@@ -87,19 +92,46 @@
     for k in range(1, cols):
         pl.semaphore_signal(barrier, inc=1, device_id=col_peer(k), device_id_type=MESH)
 
-    own_src = pl.ds(pl.multiple_of(row * own, own), own)
     own_tgt = pl.ds(pl.multiple_of(col * own, own), own)
+    groups = LANES // (2 * freqs)
+    part = own // groups
+
+    def slot(index, size, depth):
+        return pl.ds(pl.multiple_of(index * depth, depth), size)
+
+    def pack(block):
+        total = block[0:part, :]
+        for g in range(1, groups):
+            total = total + pltpu.roll(block[g * part : (g + 1) * part, :], g * 2 * freqs, 1)
+        return total
+
+    def unpack(block, shift):
+        parts = []
+        for g in range(groups):
+            by = (shift - g * 2 * freqs) % LANES
+            parts.append(pltpu.roll(block, by, 1) if by else block)
+        return jnp.concatenate(parts, axis=0)
+
+    wide = lax.broadcasted_iota(jnp.int32, (own, LANES), 1)
 
     square_buf[...] = jnp.zeros_like(square_buf)
     square_buf[0 : 2 * freqs, 0:own] = str_ref[...]
     square_buf[pos_at : pos_at + 3, 0:own] = cen_ref[...]
     square_buf[inv_at : inv_at + 2 * freqs, 0:own] = inv_ref[...]
     mine = jnp.transpose(square_buf[...])[0:own, :]
-    src_buf[own_src, :] = mine
-    tgt_buf[own_tgt, :] = mine
-
-    def push(stage, source, target, peer, sems, k):
-        copy = pltpu.make_async_remote_copy(
+    packed = jnp.concatenate(
+        [
+            pack(jnp.where(wide < pos_at, mine, 0.0)),
+            pack(jnp.where(wide < 8, pltpu.roll(mine, LANES - pos_at, 1), 0.0)),
+        ],
+        axis=0,
+    )
+    src_mine, tgt_mine = slot(row, 2 * part, 2 * part), slot(col, 2 * part, 2 * part)
+    src_pack[src_mine, :] = packed
+    tgt_pack[tgt_mine, :] = packed
+
+    def describe(stage, source, target, peer, sems, k):
+        return pltpu.make_async_remote_copy(
             src_ref=source,
             dst_ref=target,
             send_sem=sems[0].at[stage, k],
@@ -107,24 +139,24 @@
             device_id=peer,
             device_id_type=MESH,
         )
+
+    def push(*what):
+        copy = describe(*what)
         copy.start()
         return copy
 
     row_sems, col_sems = (send_row, recv_row), (send_col, recv_col)
     pl.semaphore_wait(barrier, rows + cols - 2)
-    done = []
     first = [
-        push(0, src_buf.at[own_src], src_buf.at[own_src], row_peer(k), row_sems, k)
+        push(0, src_pack.at[src_mine], src_pack.at[src_mine], row_peer(k), row_sems, k)
         for k in range(1, rows)
     ]
     side = [
-        push(0, tgt_buf.at[own_tgt], tgt_buf.at[own_tgt], col_peer(k), col_sems, k)
+        push(0, tgt_pack.at[tgt_mine], tgt_pack.at[tgt_mine], col_peer(k), col_sems, k)
         for k in range(1, cols)
     ]
 
-    list_buf[...] = jnp.zeros_like(list_buf)
-    list_buf[:, 0:listed] = lists_ref[...].astype(jnp.float32)
-    list_rows[...] = jnp.transpose(list_buf[...])
+    list_rows[...] = lists_ref[...].astype(jnp.float32)
 
     def count_step(block, carry):
         start = pl.multiple_of(block * own, own)
@@ -142,8 +174,18 @@
     waves = [wave_ref[f] for f in range(freqs)]
     turns = [wave * (0.5 / math.pi) for wave in waves]
 
+    def open_pack(packs, opened):
+        def open_step(block, carry):
+            both = packs[slot(block, 2 * part, 2 * part), :]
+            strength, place = unpack(both[0:part, :], 0), unpack(both[part:, :], pos_at)
+            opened[slot(block, own, own), :] = jnp.where(wide < pos_at, strength, place)
+            return carry
+
+        return open_step
+
     for copy in first:
         copy.wait_recv()
+    lax.fori_loop(0, rows, open_pack(src_pack, src_buf), 0)
 
     def field_step(step, carry):
         span = pl.ds(pl.multiple_of(step * STEP, STEP), STEP)
@@ -176,6 +218,7 @@
 
     for copy in side:
         copy.wait_recv()
+    lax.fori_loop(0, cols, open_pack(tgt_pack, tgt_buf), 0)
     src_rows[...] = jnp.transpose(src_buf[...])
     place = [src_rows[pos_at + axis : pos_at + axis + 1, :] for axis in range(3)]
 
@@ -187,10 +230,11 @@
         inverse = lax.rsqrt(squared)
         return squared * inverse, inverse
 
-    def derivative(f, distance, inverse_sq):
+    def derivative(f, distance, inverse):
+        inverse_cube = inverse * inverse * inverse
         phase = distance * waves[f]
         sine, cosine = sincos_turns(distance * turns[f])
-        return -(cosine + phase * sine) * inverse_sq, (phase * cosine - sine) * inverse_sq
+        return -(cosine + phase * sine) * inverse_cube, (phase * cosine - sine) * inverse_cube
 
     if keep:
 
@@ -198,7 +242,7 @@
             span = pl.ds(pl.multiple_of(step * STEP, STEP), STEP)
             distance, inverse = lengths(gaps(tgt_buf[span, :]))
             for f in range(freqs):
-                real, imag = derivative(f, distance, inverse * inverse)
+                real, imag = derivative(f, distance, inverse)
                 deriv_re[f, span, :] = real
                 deriv_im[f, span, :] = imag
             return carry
@@ -215,9 +259,9 @@
     misfit = jnp.sum(jnp.sum(resid * resid, axis=0, keepdims=True), axis=1, keepdims=True)
     lane = lax.broadcasted_iota(jnp.int32, (STEP, LANES), 1)
 
-    def source_step(step, carry):
-        span = pl.ds(pl.multiple_of(step * STEP, STEP), STEP)
-        total = jnp.where(lane == 2 * freqs, misfit, 0.0)
+    def source_sums(start):
+        span = pl.ds(pl.multiple_of(start, STEP), STEP)
+        total = jnp.zeros((STEP, LANES), jnp.float32)
         for f in range(freqs):
             cosine, sine = green_cos[f, span, :], green_sin[f, span, :]
             real = resid_buf[f : f + 1, :]
@@ -226,50 +270,91 @@
             sum_imag = jnp.sum(cosine * imag - sine * real, axis=1, keepdims=True)
             total = jnp.where(lane == f, sum_real, total)
             total = jnp.where(lane == freqs + f, sum_imag, total)
-        send_source[span, :] = total
+        return total
+
+    def source_block(r):
+        sums = [source_sums(r * own + step) for step in range(0, own, STEP)]
+        return pack(jnp.concatenate(sums, axis=0))
+
+    misfit_rows = jnp.broadcast_to(misfit, (part, LANES))
+
+    def source_copy(k):
+        there = slot(lax.rem(row + k, rows), 2 * part, 2 * part)
+        return describe(
+            1, send_source.at[there], recv_source.at[src_mine], row_peer(k), row_sems, k
+        )
+
+    def source_step(k, carry):
+        r = lax.rem(row + k, rows)
+        send_source[slot(r, 2 * part, 2 * part), :] = jnp.concatenate(
+            [source_block(r), misfit_rows], axis=0
+        )
+        source_copy(k).start()
         return carry
 
-    lax.fori_loop(0, sources // STEP, source_step, 0)
-    source_copies = []
-    for k in range(1, rows):
-        there = pl.ds(pl.multiple_of(lax.rem(row + k, rows) * own, own), own)
-        source_copies.append(
-            push(1, send_source.at[there], recv_source.at[own_src], row_peer(k), row_sems, k)
-        )
-    recv_source[own_src, :] = send_source[own_src, :]
+    lax.fori_loop(1, rows, source_step, 0)
+    recv_source[src_mine, :] = jnp.concatenate([source_block(row), misfit_rows], axis=0)
+    if keep:
+
+        def turn_step(step, carry):
+            span = pl.ds(pl.multiple_of(step * STEP, STEP), STEP)
+            block = tgt_buf[span, :]
+            for f in range(freqs):
+                g = freqs + f
+                real, imag = deriv_re[f, span, :], deriv_im[f, span, :]
+                t_real, t_imag = block[:, f : f + 1], block[:, g : g + 1]
+                s_real, s_imag = src_rows[f : f + 1, :], src_rows[g : g + 1, :]
+                turned_re[f, span, :] = t_real * real - t_imag * imag
+                turned_im[f, span, :] = t_real * imag + t_imag * real
+                deriv_re[f, span, :] = s_real * real - s_imag * imag
+                deriv_im[f, span, :] = s_real * imag + s_imag * real
+            return carry
+
+        lax.fori_loop(0, targets // STEP, turn_step, 0)
     base = row * targets
     vertex = lax.broadcasted_iota(jnp.int32, (targets, targets), 0) + base
     share = jnp.zeros((targets, targets), jnp.float32)
     for corner in range(4):
         share = share + jnp.where(conn_ref[corner : corner + 1, :] == vertex, 0.25, 0.0)
-    for copy in source_copies:
-        copy.wait_recv()
-    source = recv_source[0:own, :]
+    for k in range(1, rows):
+        source_copy(k).wait_recv()
+    both = recv_source[0 : 2 * part, :]
     for r in range(1, rows):
-        source = source + recv_source[r * own : (r + 1) * own, :]
-    objective = source[:, 2 * freqs : 2 * freqs + 1] / (freqs * points * rows) + 1e-06
-    obj_out[...] = objective[0:1, :]
-    source = source / objective
-    lane = lax.broadcasted_iota(jnp.int32, (own, LANES), 1)
-    low = lane < freqs
+        both = both + recv_source[r * 2 * part : (r + 1) * 2 * part, :]
+    objective = both[part : part + 1, 0:1] / (freqs * points * rows) + 1e-06
+    obj_out[...] = objective
+    source = unpack(both[0:part, :] / objective, 0)
+    low = wide < freqs
     inv_own = pltpu.roll(mine, LANES - inv_at, 1)
     inv_turn = jnp.where(low, -pltpu.roll(inv_own, LANES - freqs, 1), pltpu.roll(inv_own, freqs, 1))
     real = jnp.where(low, source, pltpu.roll(source, freqs, 1))
     imag = jnp.where(low, pltpu.roll(source, LANES - freqs, 1), source)
-    mu = jnp.where(lane < 2 * freqs, real * inv_own + imag * inv_turn, 0.0)
-    mu_src[own_src, :] = mu
-    mu_tgt[own_tgt, :] = mu
+    mu = jnp.where(wide < 2 * freqs, real * inv_own + imag * inv_turn, 0.0)
+    packed = pack(mu)
+    src_mine, tgt_mine = slot(row, part, part), slot(col, part, part)
+    mu_src_pack[src_mine, :] = packed
+    mu_tgt_pack[tgt_mine, :] = packed
     mu_copies = [
-        push(2, mu_src.at[own_src], mu_src.at[own_src], row_peer(k), row_sems, k)
+        push(2, mu_src_pack.at[src_mine], mu_src_pack.at[src_mine], row_peer(k), row_sems, k)
         for k in range(1, rows)
     ] + [
-        push(2, mu_tgt.at[own_tgt], mu_tgt.at[own_tgt], col_peer(k), col_sems, k)
+        push(2, mu_tgt_pack.at[tgt_mine], mu_tgt_pack.at[tgt_mine], col_peer(k), col_sems, k)
         for k in range(1, cols)
     ]
     square_buf[0:own, :] = mu
     adj_out[...] = jnp.transpose(square_buf[...])[0 : 2 * freqs, 0:own]
     for copy in mu_copies:
         copy.wait_recv()
+
+    def open_mu(packs, opened):
+        def open_step(block, carry):
+            opened[slot(block, own, own), :] = unpack(packs[slot(block, part, part), :], 0)
+            return carry
+
+        return open_step
+
+    lax.fori_loop(0, rows, open_mu(mu_src_pack, mu_src), 0)
+    lax.fori_loop(0, cols, open_mu(mu_tgt_pack, mu_tgt), 0)
     mu_rows[...] = jnp.transpose(mu_src[...])
     scale = 1.0 / math.sqrt(sources * cols * freqs)
     lane = lax.broadcasted_iota(jnp.int32, (STEP, LANES), 1)
@@ -282,18 +367,18 @@
         weight = jnp.zeros((STEP, sources), jnp.float32)
         for f in range(freqs):
             g = freqs + f
+            tm_real, tm_imag = tmu[:, f : f + 1], tmu[:, g : g + 1]
+            sm_real, sm_imag = mu_rows[f : f + 1, :], mu_rows[g : g + 1, :]
             if keep:
-                der_real, der_imag = deriv_re[f, span, :], deriv_im[f, span, :]
-            else:
-                der_real, der_imag = derivative(f, distance, inverse * inverse)
+                weight = weight + (tm_real * deriv_re[f, span, :] - tm_imag * deriv_im[f, span, :])
+                weight = weight + (sm_real * turned_re[f, span, :] - sm_imag * turned_im[f, span, :])
+                continue
+            der_real, der_imag = derivative(f, distance, inverse)
             t_real, t_imag = block[:, f : f + 1], block[:, g : g + 1]
-            tm_real, tm_imag = tmu[:, f : f + 1], tmu[:, g : g + 1]
             s_real, s_imag = src_rows[f : f + 1, :], src_rows[g : g + 1, :]
-            sm_real, sm_imag = mu_rows[f : f + 1, :], mu_rows[g : g + 1, :]
             prod_real = tm_real * s_real - tm_imag * s_imag + sm_real * t_real - sm_imag * t_imag
             prod_imag = tm_real * s_imag + tm_imag * s_real + sm_real * t_imag + sm_imag * t_real
             weight = weight + (prod_real * der_real - prod_imag * der_imag)
-        weight = weight * inverse
         total = jnp.zeros((STEP, LANES), jnp.float32)
         for axis in range(3):
             part = jnp.sum(weight * offset[axis], axis=1, keepdims=True)
@@ -322,8 +407,10 @@
         total = total + vert_recv[k * own : (k + 1) * own, :]
     square_buf[0:own, :] = total
     vert_out[...] = jnp.transpose(square_buf[...])[0:3, 0:own]
-    for copy in first + side + eta_copies + source_copies + mu_copies + vert_copies:
+    for copy in first + side + eta_copies + mu_copies + vert_copies:
         copy.wait_send()
+    for k in range(1, rows):
+        source_copy(k).wait_send()
 
 
 def on_device(centroids, strengths, self_inv, wavenumbers, field_pos, targets, lists, connect):
@@ -331,6 +418,7 @@
     rows, cols = lax.axis_size("row"), lax.axis_size("col")
     freqs = wavenumbers.shape[0]
     points, listed = lists.shape
+    pack_rows = 2 * own * 2 * freqs // LANES
     sources, block = rows * own, cols * own
     keep = freqs * block * sources * 8 <= 16 * 2**20
     kept = (freqs, block, sources) if keep else (1, 8, LANES)
@@ -348,22 +436,27 @@
         out_specs=(vmem, vmem, vmem),
         scratch_shapes=[
             pltpu.VMEM((LANES, LANES), f32),
+            pltpu.VMEM((rows * pack_rows, LANES), f32),
+            pltpu.VMEM((cols * pack_rows, LANES), f32),
             pltpu.VMEM((sources, LANES), f32),
             pltpu.VMEM((block, LANES), f32),
             pltpu.VMEM((LANES, sources), f32),
-            pltpu.VMEM((points, LANES), f32),
-            pltpu.VMEM((LANES, points), f32),
+            pltpu.VMEM((listed, points), f32),
             pltpu.VMEM((sources, points), f32),
             pltpu.VMEM((freqs, sources, points), f32),
             pltpu.VMEM((freqs, sources, points), f32),
             pltpu.VMEM((2 * freqs, 8, points), f32),
             pltpu.VMEM((cols, 2 * freqs, points), f32),
             pltpu.VMEM((2 * freqs, points), f32),
-            pltpu.VMEM((sources, LANES), f32),
-            pltpu.VMEM((sources, LANES), f32),
+            pltpu.VMEM((rows * pack_rows, LANES), f32),
+            pltpu.VMEM((rows * pack_rows, LANES), f32),
+            pltpu.VMEM((rows * pack_rows // 2, LANES), f32),
+            pltpu.VMEM((cols * pack_rows // 2, LANES), f32),
             pltpu.VMEM((sources, LANES), f32),
             pltpu.VMEM((block, LANES), f32),
             pltpu.VMEM((LANES, sources), f32),
+            pltpu.VMEM(kept, f32),
+            pltpu.VMEM(kept, f32),
             pltpu.VMEM(kept, f32),
             pltpu.VMEM(kept, f32),
             pltpu.VMEM((block, LANES), f32),
@@ -377,7 +470,7 @@
         compiler_params=pltpu.CompilerParams(
             collective_id=0, has_side_effects=True, vmem_limit_bytes=52 * 2**20
         ),
-    )(centroids, strengths, self_inv, wavenumbers, field_pos, targets, lists, connect)
+    )(centroids, strengths, self_inv, wavenumbers, field_pos, targets, lists.T, connect)
     return adjoint, vertex, objective.reshape(())
 
 

time: 44.7 us -> 47.4 us (1.060)
  local copies, waits for them, and re-layouts: 2.19 us -> 6.91 us
  Pallas kernels: 39.9 us -> 37.6 us
    unnamed x17 -> x18, local copies, waits for them, and re-layouts: 2.19 us -> 6.91 us
    pallas_call x1, Pallas kernels: 39.9 us -> 37.6 us  [on_device(): pl.pallas_call(functools.partial(kernel, (rows, cols, own, freqs, points,...]
where the time goes in v2:
time: 47.4 us; the launch traced here: 46.9 us
  Pallas kernels  37.6 us (79%)
  local copies, waits for them, and re-layouts  6.91 us (15%)
  between operations  2.47 us (5%)
    pallas_call x1, Pallas kernels, on_device(): pl.pallas_call(functools.partial(kernel, (rows, cols, own, freqs, points,...  37.6 us
    unnamed x18, local copies, waits for them, and re-layouts  6.91 us

profile of v2, /device:TPU:0, one launch (start us, length us, event | category | flops | bytes accessed | tf_op | source)
XLA Modules:
  0.0 46.9 jit_solution(3637618698444240191)
XLA Ops:
  0.6 0.0 copy-start.7
  0.6 0.6 %copy-done.7 = f32[16]{0:T(128)S(1)} copy-done((f32[16]{0:T(128)S(1)}, f32[16]{0:T(128)}, u32[]{:S(2)}) %copy-start.7) | copy-done | bytes 88
  1.3 0.0 copy-start
  1.3 0.8 %copy-done = s32[256,64]{0,1:T(8,128)S(1)} copy-done((s32[256,64]{0,1:T(8,128)S(1)}, s32[256,64]{0,1:T(8,128)}, u32[]{:S(2)}) %copy-start) | copy-done | bytes 65560
  2.1 0.0 copy-start.1
  2.1 0.8 %copy-done.1 = f32[32,256]{1,0:T(8,128)S(1)} copy-done((f32[32,256]{1,0:T(8,128)S(1)}, f32[32,256]{1,0:T(8,128)}, u32[]{:S(2)}) %copy-start.1) | copy-done | bytes 32792
  2.9 0.0 copy-start.2
  2.9 0.7 %copy-done.2 = f32[32,32]{1,0:T(8,128)S(1)} copy-done((f32[32,32]{1,0:T(8,128)S(1)}, f32[32,32]{1,0:T(8,128)}, u32[]{:S(2)}) %copy-start.2) | copy-done | bytes 4120
  3.6 0.0 copy-start.3
  3.6 0.7 %copy-done.3 = f32[32,32]{1,0:T(8,128)S(1)} copy-done((f32[32,32]{1,0:T(8,128)S(1)}, f32[32,32]{1,0:T(8,128)}, u32[]{:S(2)}) %copy-start.3) | copy-done | bytes 4120
  4.3 0.0 copy-start.4
  4.3 0.7 %copy-done.4 = f32[3,256]{1,0:T(4,128)S(1)} copy-done((f32[3,256]{1,0:T(4,128)S(1)}, f32[3,256]{1,0:T(4,128)}, u32[]{:S(2)}) %copy-start.4) | copy-done | bytes 3096
  5.0 0.0 copy-start.5
  5.0 0.7 %copy-done.5 = f32[3,32]{1,0:T(4,128)S(1)} copy-done((f32[3,32]{1,0:T(4,128)S(1)}, f32[3,32]{1,0:T(4,128)}, u32[]{:S(2)}) %copy-start.5) | copy-done | bytes 408
  5.7 0.0 copy-start.6
  5.7 0.7 %copy-done.6 = s32[4,128]{1,0:T(4,128)S(1)} copy-done((s32[4,128]{1,0:T(4,128)S(1)}, s32[4,128]{1,0:T(4,128)}, u32[]{:S(2)}) %copy-start.6) | copy-done | bytes 2072
  6.4 37.6 %shard_map.103 = (f32[32,32]{1,0:T(8,128)S(1)}, f32[3,32]{1,0:T(4,128)S(1)}, f32[1,1]{1,0:T(1,128)}) custom-call(f32[3,32]{1,0:T(4,128)S(1)} %copy-done.5, f32[32,32]{1,0:T(8,128)S(1)} %copy-done.2, f32[32,32]{1,0:T(8,128)S(1)} %copy-done.3, f32[16]{0:T(128)S(1)} %copy-done.7, f32[3,256]{1,0:T(4,128)S(1)} %copy-done.4, f32[32,256]{1,0:T(8,128)S(1)} %copy-done.1, ...), custom_call_target="tpu_custom_call" | custom-call | tf_op jit(solution)/shard_map/pallas_call | solution.py:428
  43.9 0.6 %copy.14 = f32[32,32]{1,0:T(8,128)} copy(f32[32,32]{1,0:T(8,128)S(1)} %get-tuple-element.12) | data formatting | bytes 8192
  44.6 0.6 %copy.15 = f32[3,32]{1,0:T(4,128)} copy(f32[3,32]{1,0:T(4,128)S(1)} %get-tuple-element.13) | data formatting | bytes 768
Async XLA Ops:
  0.6 0.7 %copy-start.7 = (f32[16]{0:T(128)S(1)}, f32[16]{0:T(128)}, u32[]{:S(2)}) copy-start(f32[16]{0:T(128)} %wave_ref.1) | copy-start | bytes 196
  1.3 0.8 %copy-start = (s32[256,64]{0,1:T(8,128)S(1)}, s32[256,64]{0,1:T(8,128)}, u32[]{:S(2)}) copy-start(s32[256,64]{0,1:T(8,128)} %param.14) | copy-start | bytes 196612
  2.1 0.8 %copy-start.1 = (f32[32,256]{1,0:T(8,128)S(1)}, f32[32,256]{1,0:T(8,128)}, u32[]{:S(2)}) copy-start(f32[32,256]{1,0:T(8,128)} %targ_ref.1) | copy-start | bytes 98308
  2.9 0.7 %copy-start.2 = (f32[32,32]{1,0:T(8,128)S(1)}, f32[32,32]{1,0:T(8,128)}, u32[]{:S(2)}) copy-start(f32[32,32]{1,0:T(8,128)} %str_ref.1) | copy-start | bytes 12292
  3.6 0.7 %copy-start.3 = (f32[32,32]{1,0:T(8,128)S(1)}, f32[32,32]{1,0:T(8,128)}, u32[]{:S(2)}) copy-start(f32[32,32]{1,0:T(8,128)} %inv_ref.1) | copy-start | bytes 12292
  4.3 0.7 %copy-start.4 = (f32[3,256]{1,0:T(4,128)S(1)}, f32[3,256]{1,0:T(4,128)}, u32[]{:S(2)}) copy-start(f32[3,256]{1,0:T(4,128)} %field_ref.1) | copy-start | bytes 9220
  5.0 0.7 %copy-start.5 = (f32[3,32]{1,0:T(4,128)S(1)}, f32[3,32]{1,0:T(4,128)}, u32[]{:S(2)}) copy-start(f32[3,32]{1,0:T(4,128)} %cen_ref.1) | copy-start | bytes 1156
  5.7 0.7 %copy-start.6 = (s32[4,128]{1,0:T(4,128)S(1)}, s32[4,128]{1,0:T(4,128)}, u32[]{:S(2)}) copy-start(s32[4,128]{1,0:T(4,128)} %conn_ref.1) | copy-start | bytes 6148

commit v3 on v2

--- a/solution.py
+++ b/solution.py
@@ -32,14 +32,14 @@
 
 def kernel(
     dims,
-    cen_ref,
-    str_ref,
-    inv_ref,
+    cen_hbm,
+    str_hbm,
+    inv_hbm,
     wave_ref,
-    field_ref,
-    targ_ref,
-    lists_ref,
-    conn_ref,
+    field_hbm,
+    targ_hbm,
+    lists_hbm,
+    conn_hbm,
     adj_out,
     vert_out,
     obj_out,
@@ -74,11 +74,36 @@
     recv_row,
     send_col,
     recv_col,
+    cen_ref,
+    str_ref,
+    inv_ref,
+    field_ref,
+    targ_ref,
+    lists_ref,
+    conn_ref,
+    load_sem,
 ):
     rows, cols, own, freqs, points, listed, keep = dims
     sources, targets = rows * own, cols * own
     pos_at, inv_at = 2 * freqs, 2 * freqs + 8
     row, col = lax.axis_index("row"), lax.axis_index("col")
+
+    loads = [
+        pltpu.make_async_copy(there, here, load_sem.at[index])
+        for index, (there, here) in enumerate(
+            [
+                (cen_hbm, cen_ref),
+                (str_hbm, str_ref),
+                (inv_hbm, inv_ref),
+                (lists_hbm, lists_ref),
+                (field_hbm, field_ref),
+                (targ_hbm, targ_ref),
+                (conn_hbm, conn_ref),
+            ]
+        )
+    ]
+    for load in loads:
+        load.start()
 
     def row_peer(k):
         return (lax.rem(row + k, rows), col)
@@ -115,6 +140,8 @@
     wide = lax.broadcasted_iota(jnp.int32, (own, LANES), 1)
 
     square_buf[...] = jnp.zeros_like(square_buf)
+    for load in loads[:3]:
+        load.wait()
     square_buf[0 : 2 * freqs, 0:own] = str_ref[...]
     square_buf[pos_at : pos_at + 3, 0:own] = cen_ref[...]
     square_buf[inv_at : inv_at + 2 * freqs, 0:own] = inv_ref[...]
@@ -156,6 +183,8 @@
         for k in range(1, cols)
     ]
 
+    for load in loads[3:]:
+        load.wait()
     list_rows[...] = lists_ref[...].astype(jnp.float32)
 
     def count_step(block, carry):
@@ -424,6 +453,7 @@
     kept = (freqs, block, sources) if keep else (1, 8, LANES)
     f32 = jnp.float32
     vmem = pl.BlockSpec(memory_space=pltpu.VMEM)
+    hbm = pl.BlockSpec(memory_space=pltpu.HBM)
     smem = pl.BlockSpec(memory_space=pltpu.SMEM)
     adjoint, vertex, objective = pl.pallas_call(
         functools.partial(kernel, (rows, cols, own, freqs, points, listed, keep)),
@@ -432,7 +462,7 @@
             jax.ShapeDtypeStruct((3, own), f32),
             jax.ShapeDtypeStruct((1, 1), f32),
         ),
-        in_specs=[vmem, vmem, vmem, smem, vmem, vmem, vmem, vmem],
+        in_specs=[hbm, hbm, hbm, smem, hbm, hbm, hbm, hbm],
         out_specs=(vmem, vmem, vmem),
         scratch_shapes=[
             pltpu.VMEM((LANES, LANES), f32),
@@ -466,9 +496,17 @@
             pltpu.SemaphoreType.DMA((3, rows)),
             pltpu.SemaphoreType.DMA((4, cols)),
             pltpu.SemaphoreType.DMA((4, cols)),
+            pltpu.VMEM(centroids.shape, f32),
+            pltpu.VMEM(strengths.shape, f32),
+            pltpu.VMEM(self_inv.shape, f32),
+            pltpu.VMEM(field_pos.shape, f32),
+            pltpu.VMEM(targets.shape, f32),
+            pltpu.VMEM((listed, points), jnp.int32),
+            pltpu.VMEM(connect.shape, jnp.int32),
+            pltpu.SemaphoreType.DMA((7,)),
         ],
         compiler_params=pltpu.CompilerParams(
-            collective_id=0, has_side_effects=True, vmem_limit_bytes=52 * 2**20
+            collective_id=0, has_side_effects=True, vmem_limit_bytes=60 * 2**20
         ),
     )(centroids, strengths, self_inv, wavenumbers, field_pos, targets, lists.T, connect)
     return adjoint, vertex, objective.reshape(())

time: 47.4 us -> 42.4 us (0.89)
  local copies, waits for them, and re-layouts: 6.91 us -> 1.91 us
    unnamed x18 -> x4, local copies, waits for them, and re-layouts: 6.91 us -> 1.91 us
where the time goes in v3:
time: 42.4 us; the launch traced here: 42.1 us
  Pallas kernels  37.8 us (89%)
  between operations  2.39 us (6%)
  local copies, waits for them, and re-layouts  1.91 us (5%)
    pallas_call x1, Pallas kernels, on_device(): pl.pallas_call(functools.partial(kernel, (rows, cols, own, freqs, points,...  37.8 us
    unnamed x4, local copies, waits for them, and re-layouts  1.91 us

profile of v3, /device:TPU:0, one launch (start us, length us, event | category | flops | bytes accessed | tf_op | source)
XLA Modules:
  0.0 42.1 jit_solution(18446464865380247915)
XLA Ops:
  0.6 37.8 %shard_map.103 = (f32[32,32]{1,0:T(8,128)}, f32[3,32]{1,0:T(4,128)}, f32[1,1]{1,0:T(1,128)}) custom-call(f32[3,32]{1,0:T(4,128)} %cen_hbm.1, f32[32,32]{1,0:T(8,128)} %str_hbm.1, f32[32,32]{1,0:T(8,128)} %inv_hbm.1, f32[16]{0:T(128)} %wave_ref.1, f32[3,256]{1,0:T(4,128)} %field_hbm.1, f32[32,256]{1,0:T(8,128)} %targ_hbm.1, s32[64,256]{1,0:T(8,128)} %bitcast.2, ...), custom_call_target="tpu_custom_call" | custom-call | tf_op jit(solution)/shard_map/pallas_call | solution.py:458
  38.4 0.0 copy-start
  38.4 1.3 %copy.14 = f32[32,32]{1,0:T(8,128)} copy(f32[32,32]{1,0:T(8,128)} %get-tuple-element.12) | data formatting | bytes 8192
  39.8 0.0 copy-done
  39.8 0.6 %copy.15 = f32[3,32]{1,0:T(4,128)} copy(f32[3,32]{1,0:T(4,128)S(1)} %copy-done) | data formatting | bytes 768
Async XLA Ops:
  38.4 1.3 %copy-start = (f32[3,32]{1,0:T(4,128)S(1)}, f32[3,32]{1,0:T(4,128)}, u32[]{:S(2)}) copy-start(f32[3,32]{1,0:T(4,128)} %get-tuple-element.13) | copy-start | bytes 1156

commit v4 on v3

--- a/solution.py
+++ b/solution.py
@@ -11,6 +11,7 @@
 SOFT = 1.0
 LANES = 128
 STEP = 16
+UNROLL = 4
 MESH = pl.DeviceIdType.MESH
 SIN_COEF = (6.283182818550509, -41.34142139863338, 81.59618387150631, -76.58010050947591, 41.205394790207706, -12.27126223106381)
 COS_COEF = (0.999999221570582, -19.73898251610168, 64.92872660897218, -85.2723968955171, 58.7940381912709, -21.076781284621926)
@@ -50,12 +51,13 @@
     tgt_buf,
     src_rows,
     list_rows,
-    count_buf,
+    field_rows,
+    onehot,
+    pieces,
     green_cos,
     green_sin,
-    eta_acc,
     eta_buf,
-    resid_buf,
+    source_rows,
     send_source,
     recv_source,
     mu_src_pack,
@@ -185,23 +187,29 @@
 
     for load in loads[3:]:
         load.wait()
-    list_rows[...] = lists_ref[...].astype(jnp.float32)
-
-    def count_step(block, carry):
-        start = pl.multiple_of(block * own, own)
-        ids = lax.broadcasted_iota(jnp.int32, (own, points), 0) + (block * cols + col) * own
-        ids = ids.astype(jnp.float32)
-        total = jnp.zeros((own, points), jnp.float32)
-        for entry in range(listed):
-            total = total + jnp.where(list_rows[entry : entry + 1, :] == ids, 1.0, 0.0)
-        count_buf[pl.ds(start, own), :] = total
+    ids = lists_ref[...].astype(jnp.float32)
+    owner = jnp.floor((ids + 0.5) * (1.0 / own))
+    turn = jnp.floor((owner + 0.5) * (1.0 / cols))
+    place = ids - owner * own + turn * own
+    list_rows[...] = jnp.where(owner - turn * cols == col.astype(jnp.float32), place, -1.0)
+    field_rows[...] = jnp.zeros_like(field_rows)
+    field_rows[0:3, :] = field_ref[...]
+
+    def onehot_step(entry, carry):
+        places = list_rows[pl.ds(entry, 1), :]
+        for start in range(0, sources, own):
+            ids = lax.broadcasted_iota(jnp.int32, (own, points), 0) + start
+            hit = jnp.where(places == ids.astype(jnp.float32), 1.0, 0.0)
+            onehot[entry, start : start + own, :] = hit.astype(jnp.bfloat16)
         return carry
 
-    lax.fori_loop(0, rows, count_step, 0)
-    eta_acc[...] = jnp.zeros_like(eta_acc)
-    field = [field_ref[axis : axis + 1, :] for axis in range(3)]
+    lax.fori_loop(0, listed, onehot_step, 0)
     waves = [wave_ref[f] for f in range(freqs)]
     turns = [wave * (0.5 / math.pi) for wave in waves]
+    sub = lax.broadcasted_iota(jnp.int32, (freqs, points), 0)
+    turn_col = jnp.zeros((freqs, points), jnp.float32)
+    for f in range(freqs):
+        turn_col = jnp.where(sub == f, turns[f], turn_col)
 
     def open_pack(packs, opened):
         def open_step(block, carry):
@@ -215,31 +223,47 @@
     for copy in first:
         copy.wait_recv()
     lax.fori_loop(0, rows, open_pack(src_pack, src_buf), 0)
+    src_rows[...] = jnp.transpose(src_buf[...])
+    tall = pos_at + 8
+
+    def split(value, count):
+        parts = []
+        for _ in range(count):
+            part = value.astype(jnp.bfloat16)
+            parts.append(part)
+            value = value - part.astype(jnp.float32)
+        return parts
+
+    extent = lax.broadcasted_iota(jnp.int32, (tall, sources), 0)
+    values = jnp.where(extent < pos_at + 3, src_rows[0:tall, :], 0.0)
+    parts = [part.astype(jnp.float32) for part in split(values, 3)]
+    parts = [part[0:pos_at] for part in parts] + [part[pos_at:] for part in parts]
+    spare = jnp.zeros((pieces.shape[0] - 3 * tall, sources), jnp.float32)
+    pieces[...] = jnp.concatenate(parts + [spare], axis=0).astype(jnp.bfloat16)
 
     def field_step(step, carry):
-        span = pl.ds(pl.multiple_of(step * STEP, STEP), STEP)
-        block = src_buf[span, :]
-        squared = SOFT
-        for axis in range(3):
-            gap = field[axis] - block[:, pos_at + axis : pos_at + axis + 1]
-            squared = gap * gap + squared
-        inverse = lax.rsqrt(squared)
-        distance = squared * inverse
-        gain = count_buf[span, :] * inverse
-        for f in range(freqs):
-            sine, cosine = sincos_turns(distance * turns[f])
-            cosine, sine = cosine * gain, sine * gain
-            green_cos[f, span, :] = cosine
-            green_sin[f, span, :] = sine
-            real, imag = block[:, f : f + 1], block[:, freqs + f : freqs + f + 1]
-            part_real = cosine * real - sine * imag
-            part_imag = cosine * imag + sine * real
-            eta_acc[f] += jnp.sum(part_real.reshape(STEP // 8, 8, points), axis=0)
-            eta_acc[freqs + f] += jnp.sum(part_imag.reshape(STEP // 8, 8, points), axis=0)
-        return carry
-
-    lax.fori_loop(0, sources // STEP, field_step, 0)
-    eta_buf[col] = jnp.sum(eta_acc[...], axis=1)
+        eta_real, eta_imag = carry
+        for unrolled in range(UNROLL):
+            entry = step * UNROLL + unrolled
+            near = jnp.dot(pieces[...], onehot[entry], preferred_element_type=jnp.float32)
+            strength = near[0:pos_at] + near[pos_at : 2 * pos_at] + near[2 * pos_at : 3 * pos_at]
+            where = near[3 * pos_at :]
+            where = where[0:8] + where[8:16] + where[16:24]
+            gap = field_rows[...] - where
+            squared = jnp.sum(gap * gap, axis=0, keepdims=True) + SOFT
+            inverse = lax.rsqrt(squared)
+            sine, cosine = sincos_turns(turn_col * (squared * inverse))
+            cosine, sine = cosine * inverse, sine * inverse
+            green_cos[entry] = cosine
+            green_sin[entry] = sine
+            real, imag = strength[0:freqs], strength[freqs:]
+            eta_real = eta_real + (cosine * real - sine * imag)
+            eta_imag = eta_imag + (cosine * imag + sine * real)
+        return eta_real, eta_imag
+
+    zero = jnp.zeros((freqs, points), jnp.float32)
+    eta_real, eta_imag = lax.fori_loop(0, listed // UNROLL, field_step, (zero, zero))
+    eta_buf[col] = jnp.concatenate([eta_real, eta_imag], axis=0)
     eta_copies = [
         push(1, eta_buf.at[col], eta_buf.at[col], col_peer(k), col_sems, k)
         for k in range(1, cols)
@@ -248,7 +272,6 @@
     for copy in side:
         copy.wait_recv()
     lax.fori_loop(0, cols, open_pack(tgt_pack, tgt_buf), 0)
-    src_rows[...] = jnp.transpose(src_buf[...])
     place = [src_rows[pos_at + axis : pos_at + axis + 1, :] for axis in range(3)]
 
     def gaps(block):
@@ -284,26 +307,33 @@
     for k in range(1, cols):
         eta = eta + eta_buf[k]
     resid = eta - targ_ref[...]
-    resid_buf[...] = resid
     misfit = jnp.sum(jnp.sum(resid * resid, axis=0, keepdims=True), axis=1, keepdims=True)
-    lane = lax.broadcasted_iota(jnp.int32, (STEP, LANES), 1)
-
-    def source_sums(start):
-        span = pl.ds(pl.multiple_of(start, STEP), STEP)
-        total = jnp.zeros((STEP, LANES), jnp.float32)
-        for f in range(freqs):
-            cosine, sine = green_cos[f, span, :], green_sin[f, span, :]
-            real = resid_buf[f : f + 1, :]
-            imag = resid_buf[freqs + f : freqs + f + 1, :]
-            sum_real = jnp.sum(cosine * real + sine * imag, axis=1, keepdims=True)
-            sum_imag = jnp.sum(cosine * imag - sine * real, axis=1, keepdims=True)
-            total = jnp.where(lane == f, sum_real, total)
-            total = jnp.where(lane == freqs + f, sum_imag, total)
+
+    res_real, res_imag = resid[0:freqs], resid[freqs:]
+
+    def scatter_step(step, total):
+        for unrolled in range(UNROLL):
+            entry = step * UNROLL + unrolled
+            cosine, sine = green_cos[entry], green_sin[entry]
+            real = cosine * res_real + sine * res_imag
+            imag = cosine * res_imag - sine * res_real
+            terms = jnp.concatenate(split(jnp.concatenate([real, imag], axis=0), 2), axis=0)
+            total = total + lax.dot_general(
+                terms,
+                onehot[entry],
+                (((1,), (1,)), ((), ())),
+                preferred_element_type=jnp.float32,
+            )
         return total
 
+    total = jnp.zeros((4 * freqs, sources), jnp.float32)
+    total = lax.fori_loop(0, listed // UNROLL, scatter_step, total)
+    source_rows[...] = jnp.zeros_like(source_rows)
+    source_rows[0 : 2 * freqs, :] = total[0 : 2 * freqs] + total[2 * freqs :]
+    src_buf[...] = jnp.transpose(source_rows[...])
+
     def source_block(r):
-        sums = [source_sums(r * own + step) for step in range(0, own, STEP)]
-        return pack(jnp.concatenate(sums, axis=0))
+        return pack(src_buf[slot(r, own, own), :])
 
     misfit_rows = jnp.broadcast_to(misfit, (part, LANES))
 
@@ -472,12 +502,13 @@
             pltpu.VMEM((block, LANES), f32),
             pltpu.VMEM((LANES, sources), f32),
             pltpu.VMEM((listed, points), f32),
-            pltpu.VMEM((sources, points), f32),
-            pltpu.VMEM((freqs, sources, points), f32),
-            pltpu.VMEM((freqs, sources, points), f32),
-            pltpu.VMEM((2 * freqs, 8, points), f32),
+            pltpu.VMEM((8, points), f32),
+            pltpu.VMEM((listed, sources, points), jnp.bfloat16),
+            pltpu.VMEM((-(-3 * (2 * freqs + 8) // 16) * 16, sources), jnp.bfloat16),
+            pltpu.VMEM((listed, freqs, points), f32),
+            pltpu.VMEM((listed, freqs, points), f32),
             pltpu.VMEM((cols, 2 * freqs, points), f32),
-            pltpu.VMEM((2 * freqs, points), f32),
+            pltpu.VMEM((LANES, sources), f32),
             pltpu.VMEM((rows * pack_rows, LANES), f32),
             pltpu.VMEM((rows * pack_rows, LANES), f32),
             pltpu.VMEM((rows * pack_rows // 2, LANES), f32),

time: 42.4 us -> 44.7 us (1.054)
  Pallas kernels: 37.8 us -> 40.1 us
    pallas_call x1, Pallas kernels: 37.8 us -> 40.1 us  [on_device(): pl.pallas_call(functools.partial(kernel, (rows, cols, own, freqs, points,...]
where the time goes in v4:
time: 44.7 us; the launch traced here: 44.4 us
  Pallas kernels  40.1 us (90%)
  between operations  2.39 us (5%)
  local copies, waits for them, and re-layouts  1.91 us (4%)
    pallas_call x1, Pallas kernels, on_device(): pl.pallas_call(functools.partial(kernel, (rows, cols, own, freqs, points,...  40.1 us
    unnamed x4, local copies, waits for them, and re-layouts  1.91 us

profile of v4, /device:TPU:0, one launch (start us, length us, event | category | flops | bytes accessed | tf_op | source)
XLA Modules:
  0.0 44.4 jit_solution(11119998820389271204)
XLA Ops:
  0.6 40.1 %shard_map.103 = (f32[32,32]{1,0:T(8,128)}, f32[3,32]{1,0:T(4,128)}, f32[1,1]{1,0:T(1,128)}) custom-call(f32[3,32]{1,0:T(4,128)} %cen_hbm.1, f32[32,32]{1,0:T(8,128)} %str_hbm.1, f32[32,32]{1,0:T(8,128)} %inv_hbm.1, f32[16]{0:T(128)} %wave_ref.1, f32[3,256]{1,0:T(4,128)} %field_hbm.1, f32[32,256]{1,0:T(8,128)} %targ_hbm.1, s32[64,256]{1,0:T(8,128)} %bitcast.2, ...), custom_call_target="tpu_custom_call" | custom-call | tf_op jit(solution)/shard_map/pallas_call | solution.py:488
  40.7 0.0 copy-start
  40.8 1.3 %copy.14 = f32[32,32]{1,0:T(8,128)} copy(f32[32,32]{1,0:T(8,128)} %get-tuple-element.12) | data formatting | bytes 8192
  42.1 0.0 copy-done
  42.1 0.6 %copy.15 = f32[3,32]{1,0:T(4,128)} copy(f32[3,32]{1,0:T(4,128)S(1)} %copy-done) | data formatting | bytes 768
Async XLA Ops:
  40.7 1.3 %copy-start = (f32[3,32]{1,0:T(4,128)S(1)}, f32[3,32]{1,0:T(4,128)}, u32[]{:S(2)}) copy-start(f32[3,32]{1,0:T(4,128)} %get-tuple-element.13) | copy-start | bytes 1156

commit v5 on v3

--- a/solution.py
+++ b/solution.py
@@ -105,8 +105,18 @@
     for load in loads:
         load.start()
 
+    if rows & (rows - 1):
+        raise ValueError("rows")
+
+    def row_mate(k):
+        mate, bit = 0, 1
+        while bit < rows:
+            mate = mate + bit * lax.rem(lax.div(row, bit) + lax.div(k, bit), 2)
+            bit *= 2
+        return mate
+
     def row_peer(k):
-        return (lax.rem(row + k, rows), col)
+        return (row_mate(jnp.int32(k)), col)
 
     def col_peer(k):
         return (row, lax.rem(col + k, cols))
@@ -174,10 +184,14 @@
 
     row_sems, col_sems = (send_row, recv_row), (send_col, recv_col)
     pl.semaphore_wait(barrier, rows + cols - 2)
-    first = [
-        push(0, src_pack.at[src_mine], src_pack.at[src_mine], row_peer(k), row_sems, k)
-        for k in range(1, rows)
-    ]
+
+    def panel_copy(k):
+        return describe(
+            0, src_pack.at[src_mine], src_pack.at[src_mine], row_peer(k), row_sems, k
+        )
+
+    for k in range(rows - 1, 0, -1):
+        panel_copy(k).start()
     side = [
         push(0, tgt_pack.at[tgt_mine], tgt_pack.at[tgt_mine], col_peer(k), col_sems, k)
         for k in range(1, cols)
@@ -212,12 +226,9 @@
 
         return open_step
 
-    for copy in first:
-        copy.wait_recv()
-    lax.fori_loop(0, rows, open_pack(src_pack, src_buf), 0)
-
-    def field_step(step, carry):
-        span = pl.ds(pl.multiple_of(step * STEP, STEP), STEP)
+
+    def field_step(start):
+        span = pl.ds(pl.multiple_of(start, STEP), STEP)
         block = src_buf[span, :]
         squared = SOFT
         for axis in range(3):
@@ -236,9 +247,19 @@
             part_imag = cosine * imag + sine * real
             eta_acc[f] += jnp.sum(part_real.reshape(STEP // 8, 8, points), axis=0)
             eta_acc[freqs + f] += jnp.sum(part_imag.reshape(STEP // 8, 8, points), axis=0)
+
+    def field_block(r, carry):
+        open_pack(src_pack, src_buf)(r, carry)
+        for step in range(0, own, STEP):
+            field_step(r * own + step)
         return carry
 
-    lax.fori_loop(0, sources // STEP, field_step, 0)
+    def field_from(k, carry):
+        panel_copy(k).wait_recv()
+        return field_block(row_mate(k), carry)
+
+    field_block(row, 0)
+    lax.fori_loop(1, rows, field_from, 0)
     eta_buf[col] = jnp.sum(eta_acc[...], axis=1)
     eta_copies = [
         push(1, eta_buf.at[col], eta_buf.at[col], col_peer(k), col_sems, k)
@@ -276,7 +297,7 @@
                 deriv_im[f, span, :] = imag
             return carry
 
-        lax.fori_loop(0, targets // STEP, deriv_step, 0)
+        lax.fori_loop(0, targets // STEP // 2, deriv_step, 0)
 
     for copy in eta_copies:
         copy.wait_recv()
@@ -308,13 +329,14 @@
     misfit_rows = jnp.broadcast_to(misfit, (part, LANES))
 
     def source_copy(k):
-        there = slot(lax.rem(row + k, rows), 2 * part, 2 * part)
+        there = slot(row_mate(jnp.int32(k)), 2 * part, 2 * part)
         return describe(
             1, send_source.at[there], recv_source.at[src_mine], row_peer(k), row_sems, k
         )
 
-    def source_step(k, carry):
-        r = lax.rem(row + k, rows)
+    def source_step(step, carry):
+        k = rows - step
+        r = row_mate(k)
         send_source[slot(r, 2 * part, 2 * part), :] = jnp.concatenate(
             [source_block(r), misfit_rows], axis=0
         )
@@ -339,6 +361,7 @@
                 deriv_im[f, span, :] = s_real * imag + s_imag * real
             return carry
 
+        lax.fori_loop(targets // STEP // 2, targets // STEP, deriv_step, 0)
         lax.fori_loop(0, targets // STEP, turn_step, 0)
     base = row * targets
     vertex = lax.broadcasted_iota(jnp.int32, (targets, targets), 0) + base
@@ -360,14 +383,14 @@
     imag = jnp.where(low, pltpu.roll(source, LANES - freqs, 1), source)
     mu = jnp.where(wide < 2 * freqs, real * inv_own + imag * inv_turn, 0.0)
     packed = pack(mu)
-    src_mine, tgt_mine = slot(row, part, part), slot(col, part, part)
-    mu_src_pack[src_mine, :] = packed
-    mu_tgt_pack[tgt_mine, :] = packed
+    mu_row, mu_col = slot(row, part, part), slot(col, part, part)
+    mu_src_pack[mu_row, :] = packed
+    mu_tgt_pack[mu_col, :] = packed
     mu_copies = [
-        push(2, mu_src_pack.at[src_mine], mu_src_pack.at[src_mine], row_peer(k), row_sems, k)
-        for k in range(1, rows)
+        push(2, mu_src_pack.at[mu_row], mu_src_pack.at[mu_row], row_peer(k), row_sems, k)
+        for k in range(rows - 1, 0, -1)
     ] + [
-        push(2, mu_tgt_pack.at[tgt_mine], mu_tgt_pack.at[tgt_mine], col_peer(k), col_sems, k)
+        push(2, mu_tgt_pack.at[mu_col], mu_tgt_pack.at[mu_col], col_peer(k), col_sems, k)
         for k in range(1, cols)
     ]
     square_buf[0:own, :] = mu
@@ -436,9 +459,10 @@
         total = total + vert_recv[k * own : (k + 1) * own, :]
     square_buf[0:own, :] = total
     vert_out[...] = jnp.transpose(square_buf[...])[0:3, 0:own]
-    for copy in first + side + eta_copies + mu_copies + vert_copies:
+    for copy in side + eta_copies + mu_copies + vert_copies:
         copy.wait_send()
     for k in range(1, rows):
+        panel_copy(k).wait_send()
         source_copy(k).wait_send()
 
 

time: 42.4 us -> 40.1 us (0.946)
  Pallas kernels: 37.8 us -> 35.5 us
    pallas_call x1, Pallas kernels: 37.8 us -> 35.5 us  [on_device(): pl.pallas_call(functools.partial(kernel, (rows, cols, own, freqs, points,...]
where the time goes in v5:
time: 40.1 us; the launch traced here: 39.8 us
  Pallas kernels  35.5 us (89%)
  between operations  2.39 us (6%)
  local copies, waits for them, and re-layouts  1.91 us (5%)
    pallas_call x1, Pallas kernels, on_device(): pl.pallas_call(functools.partial(kernel, (rows, cols, own, freqs, points,...  35.5 us
    unnamed x4, local copies, waits for them, and re-layouts  1.91 us

profile of v5, /device:TPU:0, one launch (start us, length us, event | category | flops | bytes accessed | tf_op | source)
XLA Modules:
  0.0 39.8 jit_solution(5681690072997805106)
XLA Ops:
  0.6 35.5 %shard_map.103 = (f32[32,32]{1,0:T(8,128)}, f32[3,32]{1,0:T(4,128)}, f32[1,1]{1,0:T(1,128)}) custom-call(f32[3,32]{1,0:T(4,128)} %cen_hbm.1, f32[32,32]{1,0:T(8,128)} %str_hbm.1, f32[32,32]{1,0:T(8,128)} %inv_hbm.1, f32[16]{0:T(128)} %wave_ref.1, f32[3,256]{1,0:T(4,128)} %field_hbm.1, f32[32,256]{1,0:T(8,128)} %targ_hbm.1, s32[64,256]{1,0:T(8,128)} %bitcast.2, ...), custom_call_target="tpu_custom_call" | custom-call | tf_op jit(solution)/shard_map/pallas_call | solution.py:482
  36.1 0.0 copy-start
  36.1 1.3 %copy.14 = f32[32,32]{1,0:T(8,128)} copy(f32[32,32]{1,0:T(8,128)} %get-tuple-element.12) | data formatting | bytes 8192
  37.5 0.0 copy-done
  37.5 0.6 %copy.15 = f32[3,32]{1,0:T(4,128)} copy(f32[3,32]{1,0:T(4,128)S(1)} %copy-done) | data formatting | bytes 768
Async XLA Ops:
  36.1 1.3 %copy-start = (f32[3,32]{1,0:T(4,128)S(1)}, f32[3,32]{1,0:T(4,128)}, u32[]{:S(2)}) copy-start(f32[3,32]{1,0:T(4,128)} %get-tuple-element.13) | copy-start | bytes 1156

commit v6 on v5

--- a/solution.py
+++ b/solution.py
@@ -67,6 +67,7 @@
     deriv_im,
     turned_re,
     turned_im,
+    weight_buf,
     sens_buf,
     vert_send,
     vert_recv,
@@ -395,9 +396,6 @@
     ]
     square_buf[0:own, :] = mu
     adj_out[...] = jnp.transpose(square_buf[...])[0 : 2 * freqs, 0:own]
-    for copy in mu_copies:
-        copy.wait_recv()
-
     def open_mu(packs, opened):
         def open_step(block, carry):
             opened[slot(block, own, own), :] = unpack(packs[slot(block, part, part), :], 0)
@@ -405,8 +403,26 @@
 
         return open_step
 
+    for copy in mu_copies[rows - 1 :]:
+        copy.wait_recv()
+    lax.fori_loop(0, cols, open_mu(mu_tgt_pack, mu_tgt), 0)
+    if keep:
+
+        def first_step(step, carry):
+            span = pl.ds(pl.multiple_of(step * STEP, STEP), STEP)
+            tmu = mu_tgt[span, :]
+            weight = jnp.zeros((STEP, sources), jnp.float32)
+            for f in range(freqs):
+                g = freqs + f
+                tm_real, tm_imag = tmu[:, f : f + 1], tmu[:, g : g + 1]
+                weight = weight + (tm_real * deriv_re[f, span, :] - tm_imag * deriv_im[f, span, :])
+            weight_buf[span, :] = weight
+            return carry
+
+        lax.fori_loop(0, targets // STEP, first_step, 0)
+    for copy in mu_copies[: rows - 1]:
+        copy.wait_recv()
     lax.fori_loop(0, rows, open_mu(mu_src_pack, mu_src), 0)
-    lax.fori_loop(0, cols, open_mu(mu_tgt_pack, mu_tgt), 0)
     mu_rows[...] = jnp.transpose(mu_src[...])
     scale = 1.0 / math.sqrt(sources * cols * freqs)
     lane = lax.broadcasted_iota(jnp.int32, (STEP, LANES), 1)
@@ -416,16 +432,15 @@
         block, tmu = tgt_buf[span, :], mu_tgt[span, :]
         offset = gaps(block)
         distance, inverse = lengths(offset)
-        weight = jnp.zeros((STEP, sources), jnp.float32)
+        weight = weight_buf[span, :] if keep else jnp.zeros((STEP, sources), jnp.float32)
         for f in range(freqs):
             g = freqs + f
-            tm_real, tm_imag = tmu[:, f : f + 1], tmu[:, g : g + 1]
             sm_real, sm_imag = mu_rows[f : f + 1, :], mu_rows[g : g + 1, :]
             if keep:
-                weight = weight + (tm_real * deriv_re[f, span, :] - tm_imag * deriv_im[f, span, :])
                 weight = weight + (sm_real * turned_re[f, span, :] - sm_imag * turned_im[f, span, :])
                 continue
             der_real, der_imag = derivative(f, distance, inverse)
+            tm_real, tm_imag = tmu[:, f : f + 1], tmu[:, g : g + 1]
             t_real, t_imag = block[:, f : f + 1], block[:, g : g + 1]
             s_real, s_imag = src_rows[f : f + 1, :], src_rows[g : g + 1, :]
             prod_real = tm_real * s_real - tm_imag * s_imag + sm_real * t_real - sm_imag * t_imag
@@ -439,26 +454,37 @@
         return carry
 
     lax.fori_loop(0, targets // STEP, sens_step, 0)
-    vert_send[...] = jnp.dot(
+    vert_send[...] = lax.dot_general(
+        jnp.transpose(sens_buf[...])[0:8, :],
         share,
-        sens_buf[...],
+        (((1,), (1,)), ((), ())),
         preferred_element_type=jnp.float32,
         precision=lax.Precision.HIGHEST,
     )
-    vert_copies = []
-    for k in range(1, cols):
-        there = pl.ds(pl.multiple_of(lax.rem(col + k, cols) * own, own), own)
-        vert_copies.append(
-            push(3, vert_send.at[there], vert_recv.at[own_tgt], col_peer(k), col_sems, k)
+    per_group = LANES // own
+
+    def vert_group(c):
+        start = lax.div(c, per_group) * LANES
+        return vert_send.at[:, pl.ds(pl.multiple_of(start, LANES), LANES)]
+
+    vert_mine = slot(col, 8, 8)
+    vert_copies = [
+        push(
+            3, vert_group(lax.rem(col + k, cols)), vert_recv.at[vert_mine], col_peer(k), col_sems, k
         )
-    vert_recv[own_tgt, :] = vert_send[own_tgt, :]
+        for k in range(1, cols)
+    ]
+    vert_recv[vert_mine, :] = vert_group(col)[...]
     for copy in vert_copies:
         copy.wait_recv()
-    total = vert_recv[0:own, :]
+    total = vert_recv[0:8, :]
     for k in range(1, cols):
-        total = total + vert_recv[k * own : (k + 1) * own, :]
-    square_buf[0:own, :] = total
-    vert_out[...] = jnp.transpose(square_buf[...])[0:3, 0:own]
+        total = total + vert_recv[k * 8 : (k + 1) * 8, :]
+    place_in = lax.rem(col, per_group)
+    vertex_own = total
+    for spot in range(1, per_group):
+        vertex_own = jnp.where(place_in == spot, pltpu.roll(total, LANES - spot * own, 1), vertex_own)
+    vert_out[...] = vertex_own[0:3, 0:own]
     for copy in side + eta_copies + mu_copies + vert_copies:
         copy.wait_send()
     for k in range(1, rows):
@@ -513,9 +539,10 @@
             pltpu.VMEM(kept, f32),
             pltpu.VMEM(kept, f32),
             pltpu.VMEM(kept, f32),
+            pltpu.VMEM(kept[1:], f32),
             pltpu.VMEM((block, LANES), f32),
-            pltpu.VMEM((block, LANES), f32),
-            pltpu.VMEM((block, LANES), f32),
+            pltpu.VMEM((8, block), f32),
+            pltpu.VMEM((cols * 8, LANES), f32),
             pltpu.SemaphoreType.DMA((3, rows)),
             pltpu.SemaphoreType.DMA((3, rows)),
             pltpu.SemaphoreType.DMA((4, cols)),

time: 40.1 us -> 40.3 us (level)
  no operation moved by 1% of the time
where the time goes in v6:
time: 40.3 us; the launch traced here: 40.1 us
  Pallas kernels  35.8 us (89%)
  between operations  2.39 us (6%)
  local copies, waits for them, and re-layouts  1.91 us (5%)
    pallas_call x1, Pallas kernels, on_device(): pl.pallas_call(functools.partial(kernel, (rows, cols, own, freqs, points,...  35.8 us
    unnamed x4, local copies, waits for them, and re-layouts  1.91 us

profile of v6, /device:TPU:0, one launch (start us, length us, event | category | flops | bytes accessed | tf_op | source)
XLA Modules:
  0.0 40.1 jit_solution(95519485470307544)
XLA Ops:
  0.6 35.8 %shard_map.103 = (f32[32,32]{1,0:T(8,128)}, f32[3,32]{1,0:T(4,128)}, f32[1,1]{1,0:T(1,128)}) custom-call(f32[3,32]{1,0:T(4,128)} %cen_hbm.1, f32[32,32]{1,0:T(8,128)} %str_hbm.1, f32[32,32]{1,0:T(8,128)} %inv_hbm.1, f32[16]{0:T(128)} %wave_ref.1, f32[3,256]{1,0:T(4,128)} %field_hbm.1, f32[32,256]{1,0:T(8,128)} %targ_hbm.1, s32[64,256]{1,0:T(8,128)} %bitcast.2, ...), custom_call_target="tpu_custom_call" | custom-call | tf_op jit(solution)/shard_map/pallas_call | solution.py:508
  36.4 0.0 copy-start
  36.4 1.3 %copy.14 = f32[32,32]{1,0:T(8,128)} copy(f32[32,32]{1,0:T(8,128)} %get-tuple-element.12) | data formatting | bytes 8192
  37.7 0.0 copy-done
  37.7 0.6 %copy.15 = f32[3,32]{1,0:T(4,128)} copy(f32[3,32]{1,0:T(4,128)S(1)} %copy-done) | data formatting | bytes 768
Async XLA Ops:
  36.4 1.3 %copy-start = (f32[3,32]{1,0:T(4,128)S(1)}, f32[3,32]{1,0:T(4,128)}, u32[]{:S(2)}) copy-start(f32[3,32]{1,0:T(4,128)} %get-tuple-element.13) | copy-start | bytes 1156

commit v7 on v6

--- a/solution.py
+++ b/solution.py
@@ -40,8 +40,7 @@
     targ_hbm,
     lists_hbm,
     conn_hbm,
-    adj_out,
-    vert_out,
+    both_out,
     obj_out,
     square_buf,
     src_pack,
@@ -395,7 +394,7 @@
         for k in range(1, cols)
     ]
     square_buf[0:own, :] = mu
-    adj_out[...] = jnp.transpose(square_buf[...])[0 : 2 * freqs, 0:own]
+    both_out[0 : 2 * freqs, :] = jnp.transpose(square_buf[...])[0 : 2 * freqs, 0:own]
     def open_mu(packs, opened):
         def open_step(block, carry):
             opened[slot(block, own, own), :] = unpack(packs[slot(block, part, part), :], 0)
@@ -484,7 +483,7 @@
     vertex_own = total
     for spot in range(1, per_group):
         vertex_own = jnp.where(place_in == spot, pltpu.roll(total, LANES - spot * own, 1), vertex_own)
-    vert_out[...] = vertex_own[0:3, 0:own]
+    both_out[2 * freqs :, :] = vertex_own[0:8, 0:own]
     for copy in side + eta_copies + mu_copies + vert_copies:
         copy.wait_send()
     for k in range(1, rows):
@@ -505,15 +504,14 @@
     vmem = pl.BlockSpec(memory_space=pltpu.VMEM)
     hbm = pl.BlockSpec(memory_space=pltpu.HBM)
     smem = pl.BlockSpec(memory_space=pltpu.SMEM)
-    adjoint, vertex, objective = pl.pallas_call(
+    both, objective = pl.pallas_call(
         functools.partial(kernel, (rows, cols, own, freqs, points, listed, keep)),
         out_shape=(
-            jax.ShapeDtypeStruct((2 * freqs, own), f32),
-            jax.ShapeDtypeStruct((3, own), f32),
+            jax.ShapeDtypeStruct((2 * freqs + 8, own), f32),
             jax.ShapeDtypeStruct((1, 1), f32),
         ),
         in_specs=[hbm, hbm, hbm, smem, hbm, hbm, hbm, hbm],
-        out_specs=(vmem, vmem, vmem),
+        out_specs=(vmem, vmem),
         scratch_shapes=[
             pltpu.VMEM((LANES, LANES), f32),
             pltpu.VMEM((rows * pack_rows, LANES), f32),
@@ -560,7 +558,7 @@
             collective_id=0, has_side_effects=True, vmem_limit_bytes=60 * 2**20
         ),
     )(centroids, strengths, self_inv, wavenumbers, field_pos, targets, lists.T, connect)
-    return adjoint, vertex, objective.reshape(())
+    return both[: 2 * freqs], both[2 * freqs : 2 * freqs + 3], objective.reshape(())
 
 
 def solution(mesh):

time: 40.3 us -> 41.1 us (1.020)
  local copies, waits for them, and re-layouts: 1.91 us -> 2.57 us
    slice x0 -> x2, local copies, waits for them, and re-layouts: none -> 2.57 us  [the longest x1 1.32 us: on_device(): both[:2 * freqs]]
    unnamed x4 -> x0, local copies, waits for them, and re-layouts: 1.91 us -> none
where the time goes in v7:
time: 41.1 us; the launch traced here: 40.7 us
  Pallas kernels  35.8 us (87%)
  local copies, waits for them, and re-layouts  2.57 us (6%)
  between operations  2.4 us (6%)
    pallas_call x1, Pallas kernels, on_device(): pl.pallas_call(functools.partial(kernel, (rows, cols, own, freqs, points,...  35.8 us
    slice x1, local copies, waits for them, and re-layouts, on_device(): both[:2 * freqs]  1.32 us
    slice x1, local copies, waits for them, and re-layouts, on_device(): both[2 * freqs:2 * freqs + 3]  1.25 us

profile of v7, /device:TPU:0, one launch (start us, length us, event | category | flops | bytes accessed | tf_op | source)
XLA Modules:
  0.0 40.7 jit_solution(2297670073925797866)
XLA Ops:
  0.6 35.8 %shard_map.103 = (f32[40,32]{1,0:T(8,128)}, f32[1,1]{1,0:T(1,128)}) custom-call(f32[3,32]{1,0:T(4,128)} %cen_hbm.1, f32[32,32]{1,0:T(8,128)} %str_hbm.1, f32[32,32]{1,0:T(8,128)} %inv_hbm.1, f32[16]{0:T(128)} %wave_ref.1, f32[3,256]{1,0:T(4,128)} %field_hbm.1, f32[32,256]{1,0:T(8,128)} %targ_hbm.1, s32[64,256]{1,0:T(8,128)} %bitcast.2, s32[4,128]{1,0:T(4,128)} %conn_hbm.1), custom_call_target="tpu_custom_call" | custom-call | tf_op jit(solution)/shard_map/pallas_call | solution.py:507
  36.4 1.2 %slice.7 = f32[3,32]{1,0:T(4,128)} slice(f32[40,32]{1,0:T(8,128)} %get-tuple-element.5), slice={[32:35], [0:32]} | slice | bytes 768 | tf_op jit(solution)/shard_map/slice | solution.py:561
  37.7 1.3 %slice.6 = f32[32,32]{1,0:T(8,128)} slice(f32[40,32]{1,0:T(8,128)} %get-tuple-element.5), slice={[0:32], [0:32]} | slice | bytes 8192 | tf_op jit(solution)/shard_map/slice | solution.py:561
